TPU v7x, 128 devices: a whole 4x4x4 slice. The times are simulated.
128 devices in a mesh: section: 2 (over x_hi), dp: 32 (over z, y, x_lo), mp: 2 (over core).
Axes of the slice: x: 4 (x_hi: 2, x_lo: 2; x = x_hi * 2 + x_lo), y: 4, z: 4, core: 2. Of those that a mesh axis runs over, the one named last changes fastest.
Arguments:
- saved_input: bfloat16 [2, 2, 8192, 4096], P('section', None, 'dp', 'mp')
- out_grad: bfloat16 [2, 8192, 4096], P(None, 'dp', 'mp'), may hold values from -6 to 6
- master_weight: float32 [2, 4096, 4096], P('section', 'mp', 'dp'), may hold values from -0.09375 to 0.09375
- moment1: float32 [2, 4096, 4096], P('section', 'mp', 'dp'), may hold values from -2 to 2
- moment2: float32 [2, 4096, 4096], P('section', 'mp', 'dp'), may hold values from 0.01 to 1
Outputs:
- input_grad: bfloat16 [2, 2, 8192, 4096], P('section', None, 'dp', 'mp')
- new_weight: float32 [2, 4096, 4096], P('section', 'mp', 'dp')
- new_moment1: float32 [2, 4096, 4096], P('section', 'mp', 'dp')
- new_moment2: float32 [2, 4096, 4096], P('section', 'mp', 'dp')
All inputs are finite; a program needn't handle non-finite values.
Results may differ from a plain program's by a relative error of at most 0.0054.
Values may be sent and summed in bfloat16 or wider, within the bound.
A program may use at most 256 MiB of HBM per device.

v0:
```python
import jax
import jax.numpy as jnp
from jax import lax
from jax.sharding import PartitionSpec as P


def from_behind(block, axis, distance):
    devices = range(lax.axis_size(axis))
    route = [(i - distance, i) for i in devices if i - distance in devices]
    return lax.ppermute(block, axis, route)


def per_device(saved_input, out_grad, master_weight, moment1, moment2):
    sections = lax.axis_size("section")
    position = lax.axis_index("section")
    topmost = position == sections - 1
    weight_rows = lax.all_gather(master_weight[0].astype(jnp.bfloat16), "dp", axis=1, tiled=True)
    activations = saved_input[0]
    grad_local = out_grad
    for step_number in range(sections):
        features = lax.all_gather(grad_local, "mp", axis=2, tiled=True)
        backward_term = jnp.einsum(
            "mtj,ij->mti", features, weight_rows, preferred_element_type=jnp.float32
        )
        layer_grad = (grad_local.astype(jnp.float32) + backward_term).astype(jnp.bfloat16)
        if step_number + 1 < sections:
            arrived = from_behind(layer_grad, "section", -1)
            grad_local = jnp.where(topmost, out_grad, arrived)
    reduced = lax.psum_scatter(
        jnp.einsum("mtj,mti->ji", features, activations, preferred_element_type=jnp.float32),
        "dp",
        scatter_dimension=0,
        tiled=True,
    )
    grad_shard = reduced.T
    total_squares = lax.psum(jnp.sum(grad_shard * grad_shard), ("section", "dp", "mp"))
    entries = float(sections * features.shape[2] * features.shape[2])
    rms_value = jnp.sqrt(total_squares / entries)
    clip_factor = jnp.minimum(1.0, 1.0 / (rms_value + 1e-06))
    clipped = clip_factor * grad_shard
    master = master_weight[0]
    new_moment1 = 0.9 * moment1[0] + 0.1 * clipped
    new_moment2 = 0.95 * moment2[0] + 0.05 * clipped * clipped
    first_fix = 1.0 - 0.9**10
    second_fix = 1.0 - 0.95**10
    update = new_moment1 / first_fix / (jnp.sqrt(new_moment2 / second_fix) + 1e-08)
    new_weight = master - 0.01 * (update + 0.1 * master)
    return (layer_grad[None], new_weight[None], new_moment1[None], new_moment2[None])


def solution(mesh):
    return jax.shard_map(
        per_device,
        mesh=mesh,
        in_specs=(
            P("section", None, "dp", "mp"),
            P(None, "dp", "mp"),
            P("section", "mp", "dp"),
            P("section", "mp", "dp"),
            P("section", "mp", "dp"),
        ),
        out_specs=(
            P("section", None, "dp", "mp"),
            P("section", "mp", "dp"),
            P("section", "mp", "dp"),
            P("section", "mp", "dp"),
        ),
        check_vma=False,
    )
```

profile of v0, /device:TPU:6, one launch (start us, length us, event | category | flops | bytes accessed | tf_op | source)
XLA Modules:
  0.0 1297.2 jit_solution(5572745190703864744)
XLA Ops:
  7.2 0.0 copy-start
  7.2 0.0 all-gather.4.cloned.1.call-start
  7.2 0.7 all-gather.4.cloned.1.call-update
  7.9 0.0 all-gather.6.cloned.1.call-start
  8.0 2.1 bitcast_convert_fusion
  10.0 0.0 all-gather.6.cloned.1.call-update
  10.1 0.0 all-gather.8.cloned.1.call-start
  10.1 18.4 %all-gather.4.cloned.1.call-done = bf16[2,256,4096]{2,1,0:T(8,128)(2,1)} async-done(((bf16[2,256,2048]{2,1,0:T(8,128)(2,1)}), bf16[2,256,4096]{2,1,0:T(8,128)(2,1)}) %all-gather.4.cloned.1.call-update) | async-done | bytes 4194320 | tf_op jit(solution)/shard_map/all_gather | solution.py:21
  28.5 363.0 %all-gather.6.cloned.1.call-done = bf16[2048,4096]{1,0:T(8,128)(2,1)} async-done(((bf16[2048,128]{1,0:T(8,128)(2,1)}), bf16[2048,4096]{1,0:T(8,128)(2,1)}) %all-gather.6.cloned.1.call-update) | async-done | bytes 16777232 | tf_op jit(solution)/shard_map/all_gather | solution.py:17
  391.5 14.9 %add_convert_fusion.1 = bf16[2,256,2048]{2,1,0:T(8,128)(2,1)} fusion(bf16[2,256,2048]{2,1,0:T(8,128)(2,1)} %param.6, bf16[2,256,4096]{2,1,0:T(8,128)(2,1)} %all-gather.4.cloned.1.call-done, bf16[2048,4096]{1,0:T(8,128)(2,1)} %all-gather.6.cloned.1.call-done), kind=kOutput, calls=%fused_computation.6 | convolution fusion | flops 8593080320 | bytes 25165824 | tf_op jit(solution)/shard_map/mtj,ij->mti/dot_general | solution.py:22
  406.4 4.4 collective-permute-start
  410.8 43.8 %collective-permute-done = bf16[2,256,2048]{2,1,0:T(8,128)(2,1)} collective-permute-done((bf16[2,256,2048]{2,1,0:T(8,128)(2,1)}, bf16[2,256,2048]{2,1,0:T(8,128)(2,1)}, u32[]{:S(2)}, u32[]{:S(2)}) %collective-permute-start) | collective-permute-done | bytes 2097184 | tf_op jit(solution)/shard_map/ppermute | solution.py:10
  454.7 3.1 broadcast_select_fusion
  457.8 0.0 all-gather.8.cloned.1.call-update
  457.8 0.2 reduce-scatter.2.cloned.1.call-start
  458.0 18.4 %all-gather.8.cloned.1.call-done = bf16[2,256,4096]{2,1,0:T(8,128)(2,1)} async-done(((bf16[2,256,2048]{2,1,0:T(8,128)(2,1)}), bf16[2,256,4096]{2,1,0:T(8,128)(2,1)}) %all-gather.8.cloned.1.call-update) | async-done | bytes 4194320 | tf_op jit(solution)/shard_map/all_gather | solution.py:21
  476.4 0.0 copy-done
  476.4 17.5 %convolution_bitcast_fusion = f32[4096,2048]{0,1:T(8,128)} fusion(bf16[2,256,4096]{2,1,0:T(8,128)(2,1)} %all-gather.8.cloned.1.call-done, bf16[1,2,256,2048]{3,2,1,0:T(8,128)(2,1)S(1)} %copy-done), kind=kOutput, calls=%fused_computation | convolution fusion | flops 8589934592 | bytes 39845888 | tf_op jit(solution)/shard_map/mtj,mti->ji/dot_general | solution.py:30
  493.9 0.0 reduce-scatter.2.cloned.1.call-update
  493.9 710.2 %reduce-scatter.2.cloned.1.call-done = f32[128,2048]{0,1:T(8,128)} async-done(((f32[4096,2048]{0,1:T(8,128)}), f32[128,2048]{0,1:T(8,128)}) %reduce-scatter.2.cloned.1.call-update) | async-done | bytes 1048592 | tf_op jit(solution)/shard_map/reduce_scatter | solution.py:29
  1204.1 2.1 multiply_reduce_fusion
  1206.2 0.0 copy-start.2
  1206.2 0.0 copy-start.1
  1206.2 15.1 %fusion.6 = bf16[1,2,256,2048]{3,2,1,0:T(8,128)(2,1)} fusion(bf16[2,256,2048]{2,1,0:T(8,128)(2,1)} %broadcast_select_fusion, bf16[2,256,4096]{2,1,0:T(8,128)(2,1)} %all-gather.8.cloned.1.call-done, bf16[2048,4096]{1,0:T(8,128)(2,1)} %all-gather.6.cloned.1.call-done), kind=kOutput, calls=%fused_computation.7 | convolution fusion | flops 8593080320 | bytes 25165824 | tf_op jit(solution)/shard_map/mtj,ij->mti/dot_general | solution.py:22
  1221.2 64.4 %psum.7 = f32[]{:T(128)} all-reduce(f32[]{:T(128)} %multiply_reduce_fusion), channel_id=1, replica_groups=mesh['section'=2,'dp'=32,'mp'=2] {'section','dp','mp'}, use_global_device_ids=true, to_apply=%region_2.3 | all-reduce | flops 1 | bytes 8 | tf_op jit(solution)/shard_map/psum | solution.py:36
  1286.4 0.0 copy-done.2
  1286.4 4.3 fusion.14
  1290.7 0.0 copy-done.1
Async XLA Ops:
  7.2 469.2 %copy-start = (bf16[1,2,256,2048]{3,2,1,0:T(8,128)(2,1)S(1)}, bf16[1,2,256,2048]{3,2,1,0:T(8,128)(2,1)}, u32[]{:S(2)}) copy-start(bf16[1,2,256,2048]{3,2,1,0:T(8,128)(2,1)} %param.5) | copy-start | bytes 6291460
  7.2 21.3 %all-gather.4.cloned.1.call-start = ((), (), s32[]{:S(2)}) async-start(), calls=%async_computation.1 | async-start | bytes 6291456 | tf_op jit(solution)/shard_map/all_gather | solution.py:21
  7.9 383.6 %all-gather.6.cloned.1.call-start = ((), (), s32[]{:S(2)}) async-start(), calls=%async_computation.2 | async-start | bytes 17301504 | tf_op jit(solution)/shard_map/all_gather | solution.py:17
  10.1 466.4 %all-gather.8.cloned.1.call-start = ((), (), s32[]{:S(2)}) async-start(), calls=%async_computation.3 | async-start | bytes 6291456 | tf_op jit(solution)/shard_map/all_gather | solution.py:21
  406.4 48.2 %collective-permute-start = (bf16[2,256,2048]{2,1,0:T(8,128)(2,1)}, bf16[2,256,2048]{2,1,0:T(8,128)(2,1)}, u32[]{:S(2)}, u32[]{:S(2)}) collective-permute-start(bf16[2,256,2048]{2,1,0:T(8,128)(2,1)} %add_convert_fusion.1), channel_id=1, source_target_pairs={{64,0},{65,1},{66,2},{67,3},{68,4},{69,5},{70,6},{71,7},{72,8},{73... | collective-permute-start | bytes 6291464 | tf_op jit(solution)/shard_map/ppermute | solution.py:10
  457.8 746.3 %reduce-scatter.2.cloned.1.call-start = ((), (), s32[]{:S(2)}) async-start(), calls=%async_computation.4 | async-start | bytes 34603008 | tf_op jit(solution)/shard_map/reduce_scatter | solution.py:29
  1206.2 80.2 %copy-start.2 = (f32[1,2048,128]{2,1,0:T(8,128)S(1)}, f32[1,2048,128]{2,1,0:T(8,128)}, u32[]{:S(2)}) copy-start(f32[1,2048,128]{2,1,0:T(8,128)} %param.7) | copy-start | bytes 3145732
  1206.2 84.5 %copy-start.1 = (bf16[1,2,256,2048]{3,2,1,0:T(8,128)(2,1)S(1)}, bf16[1,2,256,2048]{3,2,1,0:T(8,128)(2,1)}, u32[]{:S(2)}) copy-start(bf16[1,2,256,2048]{3,2,1,0:T(8,128)(2,1)} %param.5) | copy-start | bytes 6291460
Sparse Core Ops, SparseCore 0:
  9.7 18.7 all-gather.3
  30.6 360.8 all-gather.5
  457.9 18.4 all-gather.7
  494.0 709.9 reduce-scatter.1
where the time goes:
time: 1300 us
  waiting for transfers between devices  1150 us (88%)
  blocking collectives  64.4 us (5%)
  matrix products  47.5 us (4%)
  between operations  14.5 us (1%)
    reduce_scatter x1, waiting for transfers between devices, per_device(): lax.psum_scatter(jnp.einsum('mtj,mti->ji', features, activations, preferr...  710 us
    all_gather x1, waiting for transfers between devices, per_device(): lax.all_gather(master_weight[0].astype(jnp.bfloat16), 'dp', axis=1, tiled...  363 us
    psum x1, blocking collectives, per_device(): lax.psum(jnp.sum(grad_shard * grad_shard), ('section', 'dp', 'mp'))  64.4 us
    ppermute x1, waiting for transfers between devices, from_behind(): return lax.ppermute(block, axis, route)  43.8 us
    all_gather x2, waiting for transfers between devices, per_device(): features = lax.all_gather(grad_local, 'mp', axis=2, tiled=True)  36.7 us
    dot_general x2, matrix products, per_device(): jnp.einsum('mtj,ij->mti', features, weight_rows, preferred_element_type=j...  30 us
  transfers between devices with their start and end apart: 5, of which 5 were waited for; matrix products, arithmetic and copies ran while one was open for 0% of the time, Pallas kernels for 0%

commit v1 on v0

v1 whole, which is shorter than its diff:
```python
import jax
import jax.numpy as jnp
from jax import lax
from jax.experimental import pallas as pl
from jax.experimental.pallas import tpu as pltpu
from jax.sharding import PartitionSpec as P

MESH = pl.DeviceIdType.MESH
BF = jnp.bfloat16
F32 = jnp.float32
W_X, X_X, G_X, G_CUT, G_CORE, G_CORE2, G_CORE3, D_CUT, D_CORE, P_X, O_X, F_X = 0, 1, 2, 3, 4, 5, 6, 7, 11, 15, 19, 20


def dot_nt(a, b):
    return lax.dot_general(a, b, (((1,), (1,)), ((), ())), preferred_element_type=F32)


def dot_nn(a, b):
    return jnp.dot(a, b, preferred_element_type=F32)


def kernel(
    x_hbm, g_hbm, w_ref, out_ref, grad_ref, total_ref,
    Wg, Wx, Gv, D, Dp, Xo, Xp, XT, S, R1, R2, T, Tf, F, Fp, acc, Nb,
    ldx, ldg, ag_s, ag_r, rs_s, rs_r, ms, mr, ns, nr,
):
    s = lax.axis_index("section")
    d = lax.axis_index("dp")
    c = lax.axis_index("mp")
    z, y, p = d // 8, (d // 2) % 4, d % 2
    u = jnp.where(s == 1, 1 - p, p)

    def dev(s_, z_, y_, p_, c_):
        return (s_, (z_ * 4 + y_) * 2 + p_, c_)

    def zdev(o):
        return dev(s, (z + o) % 4, y, p, c)

    def ydev(o):
        return dev(s, z, (y + o) % 4, p, c)

    pair = dev(s, z, y, 1 - p, c)
    cut = dev(1 - s, z, y, 1 - p, c)
    core = dev(s, z, y, p, 1 - c)
    above = s == 1
    below = s == 0

    def rc(src, dst, i, to):
        return pltpu.make_async_remote_copy(src, dst, ms.at[i], mr.at[i], device_id=to, device_id_type=MESH)

    def xload(i):
        return pltpu.make_async_copy(x_hbm.at[:, pl.ds(128 * i, 128)], Xo.at[i // 2, i % 2], ldx.at[i])

    def gload(i, dst):
        return pltpu.make_async_copy(g_hbm.at[:, pl.ds(256 * i, 256)], dst, ldg.at[i])

    for i in range(16):
        xload(i).start()

    @pl.when(above)
    def _():
        for i in range(8):
            gload(i, Gv.at[p, 8 * c + i]).start()

    @pl.when(below)
    def _():
        for i in range(4, 8):
            gload(i, Gv.at[0, 8 + i]).start()

    @pl.when(above)
    def _():
        for r in range(8):
            Wg[z, y, p, 128 * r : 128 * r + 128] = w_ref[pl.ds(256 * r + 128 * u, 128), :].astype(BF)
            Wx[128 * r : 128 * r + 128] = w_ref[pl.ds(256 * r + 128 * (1 - u), 128), :].astype(BF)

    @pl.when(below)
    def _():
        for r in range(8):
            Wg[z, y, r // 4, 256 * (r % 4) : 256 * (r % 4) + 256] = w_ref[256 * r : 256 * r + 256, :].astype(BF)

    barrier = pltpu.get_barrier_semaphore()
    peers = [zdev(1), zdev(2), zdev(3), ydev(1), ydev(2), ydev(3), pair, cut, core]
    for to in peers:
        pl.semaphore_signal(barrier, inc=1, device_id=to, device_id_type=MESH)
    pl.semaphore_wait(barrier, len(peers))

    w_x = rc(Wx, Wg.at[z, y, p], W_X, pair)
    w_x_in = rc(Wx, Wg.at[z, y, 1 - p], W_X, pair)
    g_x = rc(Gv.at[p, pl.ds(8 * c, 4)], Gv.at[p, pl.ds(8 * c, 4)], G_X, pair)
    g_x_in = rc(Gv.at[1 - p, pl.ds(8 * c, 4)], Gv.at[1 - p, pl.ds(8 * c, 4)], G_X, pair)
    g_cut = rc(Gv.at[0, pl.ds(12, 4)], Gv.at[p, pl.ds(8 * c + 4, 4)], G_CUT, cut)
    g_cut_in = rc(Gv.at[1 - p, pl.ds(8 * c + 4, 4)], Gv.at[1 - p, pl.ds(8 * c + 4, 4)], G_CUT, cut)
    g_core = rc(Gv.at[p, pl.ds(8 * c, 8)], Gv.at[p, pl.ds(8 * c, 8)], G_CORE, core)
    g_core_in = rc(Gv.at[p, pl.ds(8 * (1 - c), 8)], Gv.at[p, pl.ds(8 * (1 - c), 8)], G_CORE, core)
    g_core2 = rc(Gv.at[1 - p, pl.ds(8 * c, 4)], Gv.at[1 - p, pl.ds(8 * c, 4)], G_CORE2, core)
    g_core2_in = rc(Gv.at[1 - p, pl.ds(8 * (1 - c), 4)], Gv.at[1 - p, pl.ds(8 * (1 - c), 4)], G_CORE2, core)
    g_core3 = rc(Gv.at[1 - p, pl.ds(8 * c + 4, 4)], Gv.at[1 - p, pl.ds(8 * c + 4, 4)], G_CORE3, core)
    g_core3_in = rc(Gv.at[1 - p, pl.ds(8 * (1 - c) + 4, 4)], Gv.at[1 - p, pl.ds(8 * (1 - c) + 4, 4)], G_CORE3, core)
    x_half = rc(Xo.at[:, 1 - u], Xp.at[:, 1 - u], X_X, pair)
    x_half_in = rc(Xo.at[:, u], Xp.at[:, u], X_X, pair)
    x_full = rc(Xo, Xp, X_X, pair)

    def ag1(k, h, o):
        block = Wg.at[z, y, h, pl.ds(256 * k, 256)]
        return pltpu.make_async_remote_copy(
            block, block, ag_s.at[0, k, h, o - 1], ag_r.at[0, k, h, o - 1],
            device_id=zdev(o) if h == 0 else ydev(o), device_id_type=MESH)

    def ag2(k, h, o):
        row = Wg.at[:, y, h, pl.ds(256 * k, 256)] if h == 0 else Wg.at[z, :, h, pl.ds(256 * k, 256)]
        return pltpu.make_async_remote_copy(
            row, row, ag_s.at[1, k, h, o - 1], ag_r.at[1, k, h, o - 1],
            device_id=ydev(o) if h == 0 else zdev(o), device_id_type=MESH)

    @pl.when(above)
    def _():
        w_x.start()
        for i in range(8):
            gload(i, Gv.at[p, 8 * c + i]).wait()
        g_core.start()
        g_x.start()
        w_x_in.wait_recv()

    @pl.when(below)
    def _():
        for i in range(4, 8):
            gload(i, Gv.at[0, 8 + i]).wait()
        g_cut.start()

    @pl.loop(0, 4)
    def _(k):
        for h in range(2):
            for o in (1, 3, 2):
                ag1(k, h, o).start()

    for i in range(16):
        xload(i).wait()

    @pl.when(above)
    def _():
        x_half.start()

    @pl.when(below)
    def _():
        x_full.start()

    @pl.loop(0, 4)
    def _(k):
        for h in range(2):
            for o in (1, 3, 2):
                ag1(k, h, o).wait_recv()
            for o in (1, 3, 2):
                ag2(k, h, o).start()

    @pl.when(above)
    def _():
        @pl.loop(0, 8)
        def _(r):
            XT[pl.ds(128 * r, 128), pl.ds(512 * p, 512)] = Xo[r, u].T

    @pl.when(below)
    def _():
        @pl.loop(0, 16)
        def _(i):
            XT[pl.ds(128 * i, 128), pl.ds(512 * p, 512)] = Xo[i // 2, i % 2].T

    @pl.when(above)
    def _():
        g_x_in.wait_recv()
        g_core2.start()
        g_cut_in.wait_recv()
        g_core3.start()
        g_core_in.wait_recv()
        g_core2_in.wait_recv()
        g_core3_in.wait_recv()

        @pl.loop(0, 4)
        def _(k):
            for h in range(2):
                for o in (1, 3, 2):
                    ag2(k, h, o).wait_recv()

            @pl.loop(0, 2)
            def _(t):
                for zz in range(4):
                    left = jnp.concatenate([Gv[t, 4 * zz + yy] for yy in range(4)], axis=1)
                    right = jnp.concatenate(
                        [Wg[zz, yy, h, pl.ds(256 * k, 256), :] for yy in range(4) for h in range(2)], axis=1)
                    part = dot_nt(left, right)
                    acc[...] = part if zz == 0 else acc[...] + part
                for rr in range(2):
                    q = 8 * c + 2 * k + rr
                    mine = Gv[t, q, :, pl.ds(128 * u, 128)].astype(F32)
                    D[q, pl.ds(512 * t, 512)] = (acc[:, 128 * rr : 128 * rr + 128] + mine).astype(BF)

            out = D.at[pl.ds(8 * c + 2 * k, 2)]
            rc(out, out, D_CUT + k, cut).start()

        rc(D.at[pl.ds(8 * c, 8), pl.ds(512 * (1 - p), 512)], Dp, O_X, pair).start()
        x_half_in.wait_recv()

        @pl.loop(0, 8)
        def _(r):
            XT[pl.ds(128 * r, 128), pl.ds(512 * (1 - p), 512)] = Xp[r, u].T

    @pl.when(below)
    def _():
        x_full.wait_recv()

        @pl.loop(0, 16)
        def _(i):
            XT[pl.ds(128 * i, 128), pl.ds(512 * (1 - p), 512)] = Xp[i // 2, i % 2].T

        @pl.loop(0, 4)
        def _(k):
            for h in range(2):
                for o in (1, 3, 2):
                    ag2(k, h, o).wait_recv()

        @pl.loop(0, 4)
        def _(k):
            got = D.at[pl.ds(8 * c + 2 * k, 2)]
            rc(got, got, D_CUT + k, cut).wait_recv()
            rc(got, got, D_CORE + k, core).start()

        @pl.loop(0, 4)
        def _(k):
            got = D.at[pl.ds(8 * (1 - c) + 2 * k, 2)]
            rc(got, got, D_CORE + k, core).wait_recv()

    def rs1(m, h, o):
        if h == 0:
            src, to = S.at[m, (z + o) % 4, :, h], zdev(o)
        else:
            src, to = S.at[m, :, (y + o) % 4, h], ydev(o)
        return pltpu.make_async_remote_copy(
            src, R1.at[m, h, o - 1], rs_s.at[0, m, h, o - 1], rs_r.at[0, m, h, o - 1],
            device_id=to, device_id_type=MESH)

    def rs2(m, h, o):
        if h == 0:
            src, to = T.at[m, h, (y + o) % 4], ydev(o)
        else:
            src, to = T.at[m, h, (z + o) % 4], zdev(o)
        return pltpu.make_async_remote_copy(
            src, R2.at[m, h, o - 1], rs_s.at[1, m, h, o - 1], rs_r.at[1, m, h, o - 1],
            device_id=to, device_id_type=MESH)

    @pl.loop(0, 4)
    def _(m):
        @pl.when(above)
        def _():
            @pl.loop(0, 16)
            def _(q):
                v = dot_nn(XT[pl.ds(256 * m, 256), 0:512], Gv[0, q])
                v = v + dot_nn(XT[pl.ds(256 * m, 256), 512:1024], Gv[1, q])
                S[m, q // 4, q % 4, 0] = v[:, :128].astype(BF)
                S[m, q // 4, q % 4, 1] = v[:, 128:].astype(BF)

        @pl.when(below)
        def _():
            @pl.loop(0, 16)
            def _(i):
                h, q = i // 8, 2 * (i % 8)
                right = jnp.concatenate([D[q], D[q + 1]], axis=1)
                v = dot_nn(XT[pl.ds(1024 * h + 256 * m, 256), 0:1024], right)
                S[m, q // 4, q % 4, h] = v[:, :128].astype(BF)
                S[m, q // 4, q % 4 + 1, h] = v[:, 128:].astype(BF)

        for h in range(2):
            for o in (1, 3, 2):
                rs1(m, h, o).start()

    def input_part(n, t):
        for zz in range(4):
            left = jnp.concatenate([D[4 * zz + yy, pl.ds(512 * t, 512)] for yy in range(4)], axis=1)
            right = jnp.concatenate(
                [Wg[zz, yy, n // 4, pl.ds(256 * (n % 4), 256), :] for yy in range(4)], axis=1)
            part = dot_nt(left, right)
            acc[...] = part if zz == 0 else acc[...] + part
        lanes = pl.ds(128 * p, 128)
        acc[:, lanes] = acc[:, lanes] + D[8 * c + n, pl.ds(512 * t, 512)].astype(F32)

    def p_x(i):
        return rc(Gv.at[0, pl.ds(2 * i, 2)], Gv.at[1, pl.ds(2 * i, 2)], P_X + i, pair)

    @pl.when(below)
    def _():
        @pl.loop(0, 4)
        def _(i):
            @pl.loop(0, 2)
            def _(j):
                input_part(2 * i + j, 1 - p)
                Gv[0, 2 * i + j] = acc[...].astype(BF)

            p_x(i).start()

    @pl.loop(0, 4)
    def _(m):
        for h in range(2):
            for o in (1, 3, 2):
                rs1(m, h, o).wait_recv()

            @pl.loop(0, 4)
            def _(b):
                own = S[m, z, b, h] if h == 0 else S[m, b, y, h]
                v = own.astype(F32)
                for o in range(3):
                    v = v + R1[m, h, o, b].astype(F32)
                T[m, h, b] = v.astype(BF)

                @pl.when(b == (y if h == 0 else z))
                def _():
                    Tf[m, h] = v

            for o in (1, 3, 2):
                rs2(m, h, o).start()

    @pl.when(below)
    def _():
        @pl.loop(0, 4)
        def _(i):
            p_x(i).wait_recv()

            @pl.loop(0, 2)
            def _(j):
                n = 2 * i + j
                input_part(n, p)
                out_ref[:, pl.ds(pl.multiple_of(256 * n, 256), 256)] = (acc[...] + Gv[1, n].astype(F32)).astype(BF)

    @pl.when(above)
    def _():
        rc(Dp, Dp, O_X, pair).wait_recv()

        @pl.loop(0, 8)
        def _(r):
            out_ref[:, pl.ds(256 * r + 128 * u, 128)] = D[8 * c + r, pl.ds(512 * p, 512)]
            out_ref[:, pl.ds(256 * r + 128 * (1 - u), 128)] = Dp[r]

    Nb[0, 0] = jnp.zeros((8, 128), F32)

    @pl.loop(0, 4)
    def _(m):
        for h in range(2):
            for o in (1, 3, 2):
                rs2(m, h, o).wait_recv()
            v = Tf[m, h]
            for o in range(3):
                v = v + R2[m, h, o].astype(F32)
            F[h, 2 * m] = v[:128]
            F[h, 2 * m + 1] = v[128:]
            Nb[0, 0] = Nb[0, 0] + jnp.sum((v * v).reshape(32, 8, 128), axis=0)

    f_x = rc(F.at[1 - p], Fp, F_X, pair)

    @pl.when(above)
    def _():
        f_x.start()

    steps = [[core], [pair], [cut], [ydev(1), ydev(3), ydev(2)], [zdev(1), zdev(3), zdev(2)]]
    for i, targets in enumerate(steps):
        copies = [
            pltpu.make_async_remote_copy(
                Nb.at[i, 0], Nb.at[i, j + 1], ns.at[i, j], nr.at[i, j], device_id=to, device_id_type=MESH)
            for j, to in enumerate(targets)]
        for copy in copies:
            copy.start()
        for copy in copies:
            copy.wait_recv()
        v = Nb[i, 0]
        for j in range(len(targets)):
            v = v + Nb[i, j + 1]
        if i + 1 < len(steps):
            Nb[i + 1, 0] = v
        else:
            total_ref[...] = v
        for copy in copies:
            copy.wait_send()

    @pl.when(above)
    def _():
        f_x.wait_recv()
        for r in range(8):
            grad_ref[2 * r + u] = F[p, r]
            grad_ref[2 * r + 1 - u] = Fp[r]

    @pl.when(below)
    def _():
        for r in range(8):
            grad_ref[r] = F[0, r]
            grad_ref[8 + r] = F[1, r]

    @pl.loop(0, 4)
    def _(k):
        for h in range(2):
            for o in (1, 3, 2):
                ag1(k, h, o).wait_send()
                ag2(k, h, o).wait_send()
                rs1(k, h, o).wait_send()
                rs2(k, h, o).wait_send()

    @pl.when(above)
    def _():
        for copy in (w_x, g_x, g_core, g_core2, g_core3, x_half, f_x):
            copy.wait_send()
        rc(Dp, Dp, O_X, pair).wait_send()

        @pl.loop(0, 4)
        def _(k):
            out = D.at[pl.ds(8 * c + 2 * k, 2)]
            rc(out, out, D_CUT + k, cut).wait_send()

    @pl.when(below)
    def _():
        g_cut.wait_send()
        x_full.wait_send()

        @pl.loop(0, 4)
        def _(k):
            out = D.at[pl.ds(8 * c + 2 * k, 2)]
            rc(out, out, D_CORE + k, core).wait_send()
            p_x(k).wait_send()


def per_device(saved_input, out_grad, master_weight, moment1, moment2):
    vmem = pl.BlockSpec(memory_space=pltpu.VMEM)
    hbm = pl.BlockSpec(memory_space=pl.ANY)
    dma = pltpu.SemaphoreType.DMA
    input_grad, grad, total = pl.pallas_call(
        kernel,
        out_shape=(
            jax.ShapeDtypeStruct((512, 2048), BF),
            jax.ShapeDtypeStruct((16, 128, 128), F32),
            jax.ShapeDtypeStruct((8, 128), F32),
        ),
        in_specs=[hbm, hbm, vmem],
        out_specs=(vmem, vmem, vmem),
        scratch_shapes=[
            pltpu.VMEM((4, 4, 2, 1024, 128), BF),
            pltpu.VMEM((1024, 128), BF),
            pltpu.VMEM((2, 16, 512, 256), BF),
            pltpu.VMEM((16, 1024, 128), BF),
            pltpu.VMEM((8, 512, 128), BF),
            pltpu.VMEM((8, 2, 512, 128), BF),
            pltpu.VMEM((8, 2, 512, 128), BF),
            pltpu.VMEM((2048, 1024), BF),
            pltpu.VMEM((4, 4, 4, 2, 256, 128), BF),
            pltpu.VMEM((4, 2, 3, 4, 256, 128), BF),
            pltpu.VMEM((4, 2, 3, 256, 128), BF),
            pltpu.VMEM((4, 2, 4, 256, 128), BF),
            pltpu.VMEM((4, 2, 256, 128), F32),
            pltpu.VMEM((2, 8, 128, 128), F32),
            pltpu.VMEM((8, 128, 128), F32),
            pltpu.VMEM((512, 256), F32),
            pltpu.VMEM((5, 4, 8, 128), F32),
            dma((16,)), dma((8,)),
            dma((2, 4, 2, 3)), dma((2, 4, 2, 3)),
            dma((2, 4, 2, 3)), dma((2, 4, 2, 3)),
            dma((21,)), dma((21,)),
            dma((5, 3)), dma((5, 3)),
        ],
        compiler_params=pltpu.CompilerParams(
            collective_id=0, has_side_effects=True, vmem_limit_bytes=62 * 2**20),
    )(saved_input.reshape(512, 2048), out_grad.reshape(512, 2048), master_weight[0])
    grad_shard = grad.reshape(2048, 128)
    total_squares = jnp.sum(total)
    rms_value = jnp.sqrt(total_squares / 33554432.0)
    clip_factor = jnp.minimum(1.0, 1.0 / (rms_value + 1e-06))
    clipped = clip_factor * grad_shard
    master = master_weight[0]
    new_moment1 = 0.9 * moment1[0] + 0.1 * clipped
    new_moment2 = 0.95 * moment2[0] + 0.05 * clipped * clipped
    first_fix = 1.0 - 0.9**10
    second_fix = 1.0 - 0.95**10
    update = new_moment1 / first_fix / (jnp.sqrt(new_moment2 / second_fix) + 1e-08)
    new_weight = master - 0.01 * (update + 0.1 * master)
    return (input_grad.reshape(1, 2, 256, 2048), new_weight[None], new_moment1[None], new_moment2[None])


def solution(mesh):
    return jax.shard_map(
        per_device,
        mesh=mesh,
        in_specs=(
            P("section", None, "dp", "mp"),
            P(None, "dp", "mp"),
            P("section", "mp", "dp"),
            P("section", "mp", "dp"),
            P("section", "mp", "dp"),
        ),
        out_specs=(
            P("section", None, "dp", "mp"),
            P("section", "mp", "dp"),
            P("section", "mp", "dp"),
            P("section", "mp", "dp"),
        ),
        check_vma=False,
    )
```

time: 1300 us -> 189 us (0.15)
  waiting for transfers between devices: 1150 us -> 0 us
  Pallas kernels: 0 us -> 181 us
  blocking collectives: 64.4 us -> 0 us
  matrix products: 47.5 us -> 0 us
  between operations: 14.5 us -> 1.44 us
    reduce_scatter x1 -> x0, waiting for transfers between devices: 710 us -> none  [per_device(): lax.psum_scatter(jnp.einsum('mtj,mti->ji', features, activations, preferr...]
    all_gather x3 -> x0, waiting for transfers between devices: 400 us -> none  [the longest x1 363 us: per_device(): lax.all_gather(master_weight[0].astype(jnp.bfloat16), 'dp', axis=1, tiled...]
    pallas_call x0 -> x1, Pallas kernels: none -> 181 us  [per_device(): pl.pallas_call(kernel, out_shape=(jax.ShapeDtypeStruct((512, 2048), BF),...]
    psum x1 -> x0, blocking collectives: 64.4 us -> none  [per_device(): lax.psum(jnp.sum(grad_shard * grad_shard), ('section', 'dp', 'mp'))]
    dot_general x3 -> x0, matrix products: 47.5 us -> none  [the longest x2 30 us: per_device(): jnp.einsum('mtj,ij->mti', features, weight_rows, preferred_element_type=j...]
    ppermute x1 -> x0, waiting for transfers between devices: 43.8 us -> none  [from_behind(): return lax.ppermute(block, axis, route)]
  transfers between devices with their start and end apart: 5 -> 0, of which waited for: 5 -> 0; matrix products, arithmetic and copies ran while one was open for 0% -> 0% of each run, Pallas kernels for 0% -> 0%
where the time goes in v1:
time: 189 us
  Pallas kernels  181 us (96%)
  other arithmetic  4.96 us (3%)
    pallas_call x1, Pallas kernels, per_device(): pl.pallas_call(kernel, out_shape=(jax.ShapeDtypeStruct((512, 2048), BF),...  181 us

profile of v1, /device:TPU:6, one launch (start us, length us, event | category | flops | bytes accessed | tf_op | source)
XLA Modules:
  0.0 189.0 jit_solution(8547251303742610021)
XLA Ops:
  0.6 0.0 copy-start.3
  0.6 181.3 %shard_map.84 = (bf16[512,2048]{1,0:T(8,128)(2,1)}, f32[16,128,128]{2,1,0:T(8,128)}, f32[8,128]{1,0:T(8,128)}) custom-call(bf16[512,2048]{1,0:T(8,128)(2,1)} %bitcast.13, bf16[512,2048]{1,0:T(8,128)(2,1)} %bitcast.14, f32[2048,128]{1,0:T(8,128)} %bitcast.11), custom_call_target="tpu_custom_call" | custom-call | tf_op jit(solution)/shard_map/pallas_call | solution.py:429
  181.9 0.0 copy-start
  181.9 0.0 copy-start.2
  181.9 1.4 reduce_sum.9
  184.1 1.3 broadcast_multiply_fusion
  185.5 0.0 copy-done.3
  185.5 0.0 copy-done
  185.5 0.0 copy-done.2
  185.5 0.0 copy-start.1
  185.5 2.2 %multiply_subtract_fusion = (f32[1,2048,128]{2,1,0:T(8,128)}, f32[1,2048,128]{2,1,0:T(8,128)}, f32[1,2048,128]{2,1,0:T(8,128)}) fusion(f32[1,2048,128]{2,1,0:T(8,128)S(1)} %copy-done, f32[1,2048,128]{2,1,0:T(8,128)S(1)} %copy-done.2, f32[1,2048,128]{2,1,0:T(8,128)S(1)} %copy-done.3, f32[1,2048,128]{2,1,0:T(8,128)S(1)} %bitcast.12), kind=kLoop, calls=%fused_computation.4 | loop fusion | flops 3932160 | bytes 7340032 | tf_op jit(solution)/shard_map/sub | solution.py:476
  187.7 0.0 copy-done.1
  187.7 1.3 copy.10
Async XLA Ops:
  0.6 184.8 %copy-start.3 = (f32[1,2048,128]{2,1,0:T(8,128)S(1)}, f32[1,2048,128]{2,1,0:T(8,128)}, u32[]{:S(2)}) copy-start(f32[1,2048,128]{2,1,0:T(8,128)} %param.9) | copy-start | bytes 3145732
  181.9 3.5 %copy-start = (f32[1,2048,128]{2,1,0:T(8,128)S(1)}, f32[1,2048,128]{2,1,0:T(8,128)}, u32[]{:S(2)}) copy-start(f32[1,2048,128]{2,1,0:T(8,128)} %param.7) | copy-start | bytes 3145732
  181.9 3.5 %copy-start.2 = (f32[1,2048,128]{2,1,0:T(8,128)S(1)}, f32[1,2048,128]{2,1,0:T(8,128)}, u32[]{:S(2)}) copy-start(f32[1,2048,128]{2,1,0:T(8,128)} %param.8) | copy-start | bytes 3145732
  185.5 2.2 %copy-start.1 = (bf16[512,2048]{1,0:T(8,128)(2,1)S(1)}, bf16[512,2048]{1,0:T(8,128)(2,1)}, u32[]{:S(2)}) copy-start(bf16[512,2048]{1,0:T(8,128)(2,1)} %get-tuple-element.7) | copy-start | bytes 6291460

commit v2 on v0

v2 whole, which is shorter than its diff:
```python
import jax
import jax.numpy as jnp
from jax import lax
from jax.experimental import pallas as pl
from jax.experimental.pallas import tpu as pltpu
from jax.sharding import PartitionSpec as P

MESH = pl.DeviceIdType.MESH
BF = jnp.bfloat16
F32 = jnp.float32
X_X, G_X, G_CUT, G_CORE, G_CORE2, G_CORE3, D_CUT, D_CORE, P_X, O_X, F_X, W_X = 0, 1, 2, 3, 4, 5, 6, 14, 22, 26, 27, 28


def dot_nt(a, b):
    return lax.dot_general(a, b, (((1,), (1,)), ((), ())), preferred_element_type=F32)


def dot_nn(a, b):
    return jnp.dot(a, b, preferred_element_type=F32)


def low_lanes(a, b):
    return jnp.where(lax.broadcasted_iota(jnp.int32, a.shape, 1) < 64, a, pltpu.roll(b, 64, 1))


def high_lanes(a, b):
    return jnp.where(lax.broadcasted_iota(jnp.int32, a.shape, 1) < 64, pltpu.roll(a, 64, 1), b)


def kernel(
    x_hbm, g_hbm, w_ref, out_ref, grad_ref,
    Wg, Wx, Gv, D, Dp, Xo, Xp, XT, S, Ra, Rb, Rc, Rd, T, Tf, F, Fp, acc, Nb,
    ldx, ldg, ag_s, ag_r, rs_s, rs_r, ms, mr, ns, nr,
):
    s = lax.axis_index("section")
    d = lax.axis_index("dp")
    c = lax.axis_index("mp")
    z, y, p = d // 8, (d // 2) % 4, d % 2
    u = jnp.where(s == 1, 1 - p, p)

    def dev(s_, z_, y_, p_, c_):
        return (s_, (z_ * 4 + y_) * 2 + p_, c_)

    def zdev(o):
        return dev(s, (z + o) % 4, y, p, c)

    def ydev(o):
        return dev(s, z, (y + o) % 4, p, c)

    pair = dev(s, z, y, 1 - p, c)
    cut = dev(1 - s, z, y, 1 - p, c)
    core = dev(s, z, y, p, 1 - c)
    near = [core, pair, cut, dev(s, z, y, 1 - p, 1 - c), dev(1 - s, z, y, 1 - p, 1 - c),
            dev(1 - s, z, y, p, c), dev(1 - s, z, y, p, 1 - c)]
    above = s == 1
    below = s == 0

    def rc(src, dst, i, to):
        return pltpu.make_async_remote_copy(src, dst, ms.at[i], mr.at[i], device_id=to, device_id_type=MESH)

    def xload(i):
        return pltpu.make_async_copy(x_hbm.at[:, pl.ds(128 * i, 128)], Xo.at[i // 2, i % 2], ldx.at[i])

    def gload(i, dst):
        return pltpu.make_async_copy(g_hbm.at[:, pl.ds(256 * i, 256)], dst, ldg.at[i])

    for i in range(16):
        xload(i).start()

    @pl.when(above)
    def _():
        for i in range(8):
            gload(i, Gv.at[p, 8 * c + i]).start()

    @pl.when(below)
    def _():
        for i in range(4, 8):
            gload(i, Gv.at[0, 8 + i]).start()

    @pl.when(above)
    def _():
        for a in range(16):
            b, r = a // 8, a % 8
            Wg[z, y, p, 64 * a : 64 * a + 64] = w_ref[pl.ds(256 * r + 128 * u + 64 * b, 64), :].astype(BF)
            Wx[64 * a : 64 * a + 64] = w_ref[pl.ds(256 * r + 128 * (1 - u) + 64 * b, 64), :].astype(BF)

    @pl.when(below)
    def _():
        for r in range(8):
            Wg[z, y, r // 4, 256 * (r % 4) : 256 * (r % 4) + 256] = w_ref[256 * r : 256 * r + 256, :].astype(BF)

    barrier = pltpu.get_barrier_semaphore()
    peers = [zdev(1), zdev(2), zdev(3), ydev(1), ydev(2), ydev(3), *near]
    for to in peers:
        pl.semaphore_signal(barrier, inc=1, device_id=to, device_id_type=MESH)
    pl.semaphore_wait(barrier, len(peers))

    def w_x(k):
        rows = pl.ds(128 * k, 128)
        return rc(Wx.at[rows], Wg.at[z, y, p, rows], W_X + k, pair)

    g_x = rc(Gv.at[p, pl.ds(8 * c, 4)], Gv.at[p, pl.ds(8 * c, 4)], G_X, pair)
    g_x_in = rc(Gv.at[1 - p, pl.ds(8 * c, 4)], Gv.at[1 - p, pl.ds(8 * c, 4)], G_X, pair)
    g_cut = rc(Gv.at[0, pl.ds(12, 4)], Gv.at[p, pl.ds(8 * c + 4, 4)], G_CUT, cut)
    g_cut_in = rc(Gv.at[1 - p, pl.ds(8 * c + 4, 4)], Gv.at[1 - p, pl.ds(8 * c + 4, 4)], G_CUT, cut)
    g_core = rc(Gv.at[p, pl.ds(8 * c, 8)], Gv.at[p, pl.ds(8 * c, 8)], G_CORE, core)
    g_core_in = rc(Gv.at[p, pl.ds(8 * (1 - c), 8)], Gv.at[p, pl.ds(8 * (1 - c), 8)], G_CORE, core)
    g_core2 = rc(Gv.at[1 - p, pl.ds(8 * c, 4)], Gv.at[1 - p, pl.ds(8 * c, 4)], G_CORE2, core)
    g_core2_in = rc(Gv.at[1 - p, pl.ds(8 * (1 - c), 4)], Gv.at[1 - p, pl.ds(8 * (1 - c), 4)], G_CORE2, core)
    g_core3 = rc(Gv.at[1 - p, pl.ds(8 * c + 4, 4)], Gv.at[1 - p, pl.ds(8 * c + 4, 4)], G_CORE3, core)
    g_core3_in = rc(Gv.at[1 - p, pl.ds(8 * (1 - c) + 4, 4)], Gv.at[1 - p, pl.ds(8 * (1 - c) + 4, 4)], G_CORE3, core)
    x_half = rc(Xo.at[:, 1 - u], Xp.at[:, 1 - u], X_X, pair)
    x_half_in = rc(Xo.at[:, u], Xp.at[:, u], X_X, pair)
    x_full = rc(Xo, Xp, X_X, pair)

    def axis(stage, h):
        return (z, zdev) if stage == h else (y, ydev)

    def gather(stage, i, k, h):
        e, to = axis(stage, h)
        e = (e, e, (e + 3) % 4, (e + 1) % 4)[i]
        rows = pl.ds(128 * k + (0, 0, 0, 64)[i], (128, 128, 64, 64)[i])
        if stage == 0:
            ref = Wg.at[e, y, h, rows] if h == 0 else Wg.at[z, e, h, rows]
        else:
            ref = Wg.at[:, e, h, rows] if h == 0 else Wg.at[e, :, h, rows]
        return pltpu.make_async_remote_copy(
            ref, ref, ag_s.at[stage, k, h, i], ag_r.at[stage, k, h, i],
            device_id=to((1, 3, 1, 3)[i]), device_id_type=MESH)

    def gather_on(stage, k):
        for h in range(2):
            for i in range(2):
                gather(stage, i, k, h).wait_recv()
                gather(stage, i + 2, k, h).start()

    def gather_end(stage, k):
        for h in range(2):
            for i in (2, 3):
                gather(stage, i, k, h).wait_recv()

    @pl.when(above)
    def _():
        for k in range(8):
            w_x(k).start()
        for i in range(8):
            gload(i, Gv.at[p, 8 * c + i]).wait()
        g_x.start()
        g_core.start()

    @pl.when(below)
    def _():
        for i in range(4, 8):
            gload(i, Gv.at[0, 8 + i]).wait()
        g_cut.start()

    def gather_begin(k):
        @pl.when(above)
        def _():
            w_x(k).wait_recv()

        for h in range(2):
            for i in range(2):
                gather(0, i, k, h).start()

    def gather_rows(k):
        for h in range(2):
            for i in range(2):
                gather(1, i, k, h).start()

    def unit(k, j):
        t = jnp.where(s == 1, p, 1 - p) if j == 0 else jnp.where(s == 1, 1 - p, p)
        return t, D.at[pl.ds(8 * c + 2 * k, 2), pl.ds(512 * t, 512)]

    def from_core(k, j):
        t = unit(k, j)[0]
        return D.at[pl.ds(8 * (1 - c) + 2 * k, 2), pl.ds(512 * t, 512)]

    def d_cut(k, j):
        ref = unit(k, j)[1]
        return rc(ref, ref, D_CUT + 2 * k + j, cut)

    def d_core(k, j):
        ref = unit(k, j)[1]
        return rc(ref, ref, D_CORE + 2 * k + j, core)

    def d_core_in(k, j):
        ref = from_core(k, j)
        return rc(ref, ref, D_CORE + 2 * k + j, core)

    def d_on(k, j):
        d_cut(k, j).wait_recv()
        d_core(k, j).start()

    def layer_unit(k, j):
        t = unit(k, j)[0]
        for zz in range(4):
            left = jnp.concatenate([Gv[t, 4 * zz + yy] for yy in range(4)], axis=1)
            right = jnp.concatenate(
                [Wg[zz, yy, h, pl.ds(256 * k, 256), :] for yy in range(4) for h in range(2)], axis=1)
            part = dot_nt(left, right)
            acc[...] = part if zz == 0 else acc[...] + part
        for rr in range(2):
            q = 8 * c + 4 * (k % 2) + 2 * rr
            g0 = Gv[t, q, :, pl.ds(128 * u, 128)].astype(F32)
            g1 = Gv[t, q + 1, :, pl.ds(128 * u, 128)].astype(F32)
            mine = jnp.where(k < 2, low_lanes(g0, g1), high_lanes(g0, g1))
            D[8 * c + 2 * k + rr, pl.ds(512 * t, 512)] = (acc[:, 128 * rr : 128 * rr + 128] + mine).astype(BF)
        d_cut(k, j).start()

    gather_begin(0)
    gather_begin(1)

    @pl.loop(0, 12)
    def _(i):
        @pl.when(i < 6)
        def _():
            gather_begin(i + 2)

        @pl.when(i < 8)
        def _():
            gather_on(0, i)

        @pl.when((i >= 1) & (i < 9))
        def _():
            gather_end(0, i - 1)
            gather_rows(i - 1)

        @pl.when((i >= 3) & (i < 11))
        def _():
            gather_on(1, i - 3)

        @pl.when(i >= 4)
        def _():
            gather_end(1, i - 4)

        @pl.when(i == 4)
        def _():
            for j in range(16):
                xload(j).wait()

            @pl.when(below)
            def _():
                x_full.start()

                @pl.loop(0, 16)
                def _(j):
                    XT[pl.ds(128 * j, 128), pl.ds(512 * p, 512)] = Xo[j // 2, j % 2].T

            @pl.when(above)
            def _():
                g_core_in.wait_recv()

                @pl.loop(0, 8)
                def _(r):
                    XT[pl.ds(128 * r, 128), pl.ds(512 * p, 512)] = Xo[r, u].T

        @pl.when(above & (i >= 5) & (i % 2 == 1))
        def _():
            k = (i - 5) // 2
            layer_unit(k, 0)

            @pl.when(k == 0)
            def _():
                g_x_in.wait_recv()
                g_core2.start()
                x_half.start()
                g_cut_in.wait_recv()
                g_core3.start()
                g_core2_in.wait_recv()
                g_core3_in.wait_recv()

            @pl.when(k < 2)
            def _():
                layer_unit(k, 1)

        @pl.when(below & ((i == 9) | (i == 11)))
        def _():
            d_on((i - 9) // 2, 0)
            d_on((i - 9) // 2, 1)

    @pl.when(above)
    def _():
        @pl.loop(2, 4)
        def _(k):
            layer_unit(k, 1)

        rc(D.at[pl.ds(8 * c, 8), pl.ds(512 * (1 - p), 512)], Dp, O_X, pair).start()
        x_half_in.wait_recv()

        @pl.loop(0, 8)
        def _(r):
            XT[pl.ds(128 * r, 128), pl.ds(512 * (1 - p), 512)] = Xp[r, u].T

    LOW, HIGH, ALL = pl.ds(0, 128), pl.ds(128, 128), pl.ds(0, 256)

    def block(stage, m, h, e, rows):
        if stage == 1:
            return T.at[m, h, e, rows]
        return S.at[m, e, :, h, rows] if h == 0 else S.at[m, :, e, h, rows]

    def reduce(stage, i, m, h):
        e, to = axis(stage, h)
        rows = (LOW, HIGH, HIGH, LOW, LOW, HIGH)[i]
        src = block(stage, m, h, (e + (2, 2, 1, 3, 1, 3)[i]) % 4, rows)
        first, second = ((Ra, Rb), (Rc, Rd))[stage]
        if i < 2:
            dst = first.at[m, h, i]
        else:
            dst = second.at[m, h, i % 2, :, rows] if stage == 0 else second.at[m, h, i % 2, rows]
        return pltpu.make_async_remote_copy(
            src, dst, rs_s.at[stage, m, h, i], rs_r.at[stage, m, h, i],
            device_id=to((1, 3)[i % 2]), device_id_type=MESH)

    def reduce_start(stage, m, h):
        for i in range(4):
            reduce(stage, i, m, h).start()

    def reduce_on(stage, m):
        for h in range(2):
            e = axis(stage, h)[0]
            for i in range(2):
                reduce(stage, i, m, h).wait_recv()
                mine = block(stage, m, h, (e + (1, 3)[i]) % 4, (LOW, HIGH)[i])
                came = (Ra, Rc)[stage].at[m, h, i]
                if stage == 0:
                    @pl.loop(0, 4)
                    def _(b):
                        mine[b] = (mine[b].astype(F32) + came[b].astype(F32)).astype(BF)
                else:
                    mine[...] = (mine[...].astype(F32) + came[...].astype(F32)).astype(BF)
                reduce(stage, i + 4, m, h).start()

    def row_sums(m):
        for h in range(2):
            for i in range(2, 6):
                reduce(0, i, m, h).wait_recv()
            mine = block(0, m, h, axis(0, h)[0], ALL)

            @pl.loop(0, 4)
            def _(b):
                v = mine[b].astype(F32) + Rb[m, h, 0, b].astype(F32) + Rb[m, h, 1, b].astype(F32)
                T[m, h, b] = v.astype(BF)

                @pl.when(b == axis(1, h)[0])
                def _():
                    Tf[m, h] = v

            reduce_start(1, m, h)

    def finish(m):
        for h in range(2):
            for i in range(2, 6):
                reduce(1, i, m, h).wait_recv()
            v = Tf[m, h] + Rd[m, h, 0].astype(F32) + Rd[m, h, 1].astype(F32)
            F[h, 2 * m] = v[:128]
            F[h, 2 * m + 1] = v[128:]
            Nb[0, 0] = Nb[0, 0] + jnp.sum((v * v).reshape(32, 8, 128), axis=0)

    def input_part(n, t):
        for zz in range(4):
            left = jnp.concatenate([Gv[t, 8 + 2 * zz], Gv[t, 9 + 2 * zz]], axis=1)
            right = jnp.concatenate(
                [Wg[zz, yy, n // 4, pl.ds(256 * (n % 4), 256), :] for yy in range(4)], axis=1)
            part = dot_nt(left, right)
            acc[...] = part if zz == 0 else acc[...] + part
        lanes = pl.ds(128 * p, 128)
        mine = Gv[t, 8 + 4 * c + n // 2, :, pl.ds(pl.multiple_of(128 * (n % 2), 128), 128)]
        acc[:, lanes] = acc[:, lanes] + mine.astype(F32)

    def p_x(i):
        return rc(Gv.at[0, pl.ds(2 * i, 2)], Gv.at[1, pl.ds(2 * i, 2)], P_X + i, pair)

    def weight_grad(m):
        @pl.loop(0, 16)
        def _(q):
            v = dot_nn(XT[pl.ds(256 * m, 256), 0:512], Gv[0, q])
            v = v + dot_nn(XT[pl.ds(256 * m, 256), 512:1024], Gv[1, q])
            S[m, q // 4, q % 4, 0] = v[:, :128].astype(BF)
            S[m, q // 4, q % 4, 1] = v[:, 128:].astype(BF)

    def weight_grad_part(k):
        @pl.loop(0, 8)
        def _(i):
            cc, m = i // 4, i % 4
            right = jnp.concatenate([D[8 * cc + 2 * k], D[8 * cc + 2 * k + 1]], axis=1)
            v = [dot_nn(XT[pl.ds(1024 * h + 256 * m, 256), 0:1024], right) for h in range(2)]
            for rr in range(2):
                v0, v1 = (a[:, 128 * rr : 128 * rr + 128] for a in v)
                to = S.at[2 * (k // 2) + m // 2, 2 * cc + k % 2]
                to[2 * rr, m % 2] = low_lanes(v0, v1).astype(BF)
                to[2 * rr + 1, m % 2] = high_lanes(v0, v1).astype(BF)

    def natural(t):
        @pl.loop(0, 8)
        def _(a):
            b0, b1 = 8 * (a // 4) + a % 4, 8 * (a // 4) + 4 + a % 4
            v0 = D[b0, pl.ds(512 * t, 512)].astype(F32)
            v1 = D[b1, pl.ds(512 * t, 512)].astype(F32)
            Gv[t, 8 + a, :, 0:128] = low_lanes(v0, v1).astype(BF)
            Gv[t, 8 + a, :, 128:256] = high_lanes(v0, v1).astype(BF)

    def partner_part(i):
        @pl.loop(0, 2)
        def _(j):
            input_part(2 * i + j, 1 - p)
            Gv[0, 2 * i + j] = acc[...].astype(BF)

        p_x(i).start()

    def first_reduce(m):
        for h in range(2):
            reduce_start(0, m, h)

    @pl.when(below)
    def _():
        x_full.wait_recv()

        @pl.loop(0, 16)
        def _(i):
            XT[pl.ds(128 * i, 128), pl.ds(512 * (1 - p), 512)] = Xp[i // 2, i % 2].T

        @pl.loop(0, 2)
        def _(k):
            d_core_in(k, 0).wait_recv()
            d_core_in(k, 1).wait_recv()
            weight_grad_part(k)

        @pl.loop(0, 2)
        def _(m):
            first_reduce(m)

        g_cut.wait_send()

        @pl.loop(2, 4)
        def _(k):
            d_on(k, 0)

        @pl.loop(2, 4)
        def _(k):
            d_core_in(k, 0).wait_recv()

        natural(1 - p)

        @pl.loop(0, 2)
        def _(i):
            partner_part(2 * i)
            partner_part(2 * i + 1)
            reduce_on(0, i)

        @pl.loop(2, 4)
        def _(k):
            d_on(k, 1)

        @pl.loop(2, 4)
        def _(k):
            d_core_in(k, 1).wait_recv()
            weight_grad_part(k)

        @pl.loop(2, 4)
        def _(m):
            first_reduce(m)

        natural(p)

    Nb[0, 0] = jnp.zeros((8, 128), F32)

    @pl.loop(0, 8)
    def _(i):
        @pl.when(above & (i < 4))
        def _():
            weight_grad(i)
            first_reduce(i)

        @pl.when((i >= 1) & (i < 5) & (above | (i >= 3)))
        def _():
            reduce_on(0, i - 1)

        @pl.when((i >= 2) & (i < 6))
        def _():
            row_sums(i - 2)

        @pl.when((i >= 3) & (i < 7))
        def _():
            reduce_on(1, i - 3)

        @pl.when(i >= 4)
        def _():
            finish(i - 4)

    f_x = rc(F.at[1 - p], Fp, F_X, pair)

    @pl.when(above)
    def _():
        f_x.start()

    def own_part(i):
        @pl.when(below)
        def _():
            p_x(i).wait_recv()

            @pl.loop(0, 2)
            def _(j):
                n = 2 * i + j
                input_part(n, p)
                out_ref[:, pl.ds(pl.multiple_of(256 * n, 256), 256)] = (acc[...] + Gv[1, n].astype(F32)).astype(BF)

    steps = [near, [ydev(1), ydev(3), ydev(2)], [zdev(1), zdev(3), zdev(2)]]
    for i, targets in enumerate(steps):
        copies = [
            pltpu.make_async_remote_copy(
                Nb.at[i, 0], Nb.at[i, j + 1], ns.at[i, j], nr.at[i, j], device_id=to, device_id_type=MESH)
            for j, to in enumerate(targets)]
        for copy in copies:
            copy.start()
        own_part(i)
        for copy in copies:
            copy.wait_recv()
        v = Nb[i, 0]
        for j in range(len(targets)):
            v = v + Nb[i, j + 1]
        if i + 1 < len(steps):
            Nb[i + 1, 0] = v
        else:
            total = v
        for copy in copies:
            copy.wait_send()
    total = jnp.broadcast_to(jnp.sum(total, keepdims=True), (8, 128))
    clip = jnp.minimum(1.0, 1.0 / (jnp.sqrt(total / 33554432.0) + 1e-06))[0:1, :]

    @pl.when(above)
    def _():
        f_x.wait_recv()
        for r in range(8):
            grad_ref[pl.ds(256 * r + 128 * u, 128), :] = F[p, r] * clip
            grad_ref[pl.ds(256 * r + 128 * (1 - u), 128), :] = Fp[r] * clip

    @pl.when(below)
    def _():
        for r in range(8):
            m, half = r // 2, r % 2
            a, b = F[m % 2, 2 * (m // 2) + half], F[m % 2, 4 + 2 * (m // 2) + half]
            grad_ref[128 * r : 128 * r + 128, :] = low_lanes(a, b) * clip
            grad_ref[1024 + 128 * r : 1152 + 128 * r, :] = high_lanes(a, b) * clip

    own_part(3)

    @pl.when(above)
    def _():
        rc(Dp, Dp, O_X, pair).wait_recv()

        @pl.loop(0, 4)
        def _(a):
            for v0, v1, par in (
                (D[8 * c + a, pl.ds(512 * p, 512)], D[8 * c + 4 + a, pl.ds(512 * p, 512)], u),
                (Dp[a], Dp[4 + a], 1 - u),
            ):
                v0, v1 = v0.astype(F32), v1.astype(F32)
                out_ref[:, pl.ds(pl.multiple_of(512 * a + 128 * par, 128), 128)] = low_lanes(v0, v1).astype(BF)
                out_ref[:, pl.ds(pl.multiple_of(512 * a + 256 + 128 * par, 128), 128)] = high_lanes(v0, v1).astype(BF)

    @pl.loop(0, 8)
    def _(k):
        for h in range(2):
            for stage in range(2):
                for i in range(4):
                    gather(stage, i, k, h).wait_send()

    @pl.loop(0, 4)
    def _(k):
        for h in range(2):
            for stage in range(2):
                for i in range(6):
                    reduce(stage, i, k, h).wait_send()

    @pl.when(above)
    def _():
        for copy in (g_x, g_core, g_core2, g_core3, x_half, f_x):
            copy.wait_send()
        for k in range(8):
            w_x(k).wait_send()
        rc(Dp, Dp, O_X, pair).wait_send()

        @pl.loop(0, 4)
        def _(k):
            d_cut(k, 0).wait_send()
            d_cut(k, 1).wait_send()

    @pl.when(below)
    def _():
        x_full.wait_send()

        @pl.loop(0, 4)
        def _(k):
            d_core(k, 0).wait_send()
            d_core(k, 1).wait_send()
            p_x(k).wait_send()


def per_device(saved_input, out_grad, master_weight, moment1, moment2):
    vmem = pl.BlockSpec(memory_space=pltpu.VMEM)
    hbm = pl.BlockSpec(memory_space=pl.ANY)
    dma = pltpu.SemaphoreType.DMA
    input_grad, clipped = pl.pallas_call(
        kernel,
        out_shape=(
            jax.ShapeDtypeStruct((512, 2048), BF),
            jax.ShapeDtypeStruct((2048, 128), F32),
        ),
        in_specs=[hbm, hbm, vmem],
        out_specs=(vmem, vmem),
        scratch_shapes=[
            pltpu.VMEM((4, 4, 2, 1024, 128), BF),
            pltpu.VMEM((1024, 128), BF),
            pltpu.VMEM((2, 16, 512, 256), BF),
            pltpu.VMEM((16, 1024, 128), BF),
            pltpu.VMEM((8, 512, 128), BF),
            pltpu.VMEM((8, 2, 512, 128), BF),
            pltpu.VMEM((8, 2, 512, 128), BF),
            pltpu.VMEM((2048, 1024), BF),
            pltpu.VMEM((4, 4, 4, 2, 256, 128), BF),
            pltpu.VMEM((4, 2, 2, 4, 128, 128), BF),
            pltpu.VMEM((4, 2, 2, 4, 256, 128), BF),
            pltpu.VMEM((4, 2, 2, 128, 128), BF),
            pltpu.VMEM((4, 2, 2, 256, 128), BF),
            pltpu.VMEM((4, 2, 4, 256, 128), BF),
            pltpu.VMEM((4, 2, 256, 128), F32),
            pltpu.VMEM((2, 8, 128, 128), F32),
            pltpu.VMEM((8, 128, 128), F32),
            pltpu.VMEM((512, 256), F32),
            pltpu.VMEM((3, 8, 8, 128), F32),
            dma((16,)), dma((8,)),
            dma((2, 8, 2, 4)), dma((2, 8, 2, 4)),
            dma((2, 4, 2, 6)), dma((2, 4, 2, 6)),
            dma((36,)), dma((36,)),
            dma((3, 7)), dma((3, 7)),
        ],
        compiler_params=pltpu.CompilerParams(
            collective_id=0, has_side_effects=True, vmem_limit_bytes=62 * 2**20),
    )(saved_input.reshape(512, 2048), out_grad.reshape(512, 2048), master_weight[0])
    master = master_weight[0]
    new_moment1 = 0.9 * moment1[0] + 0.1 * clipped
    new_moment2 = 0.95 * moment2[0] + 0.05 * clipped * clipped
    first_fix = 1.0 - 0.9**10
    second_fix = 1.0 - 0.95**10
    update = new_moment1 / first_fix / (jnp.sqrt(new_moment2 / second_fix) + 1e-08)
    new_weight = master - 0.01 * (update + 0.1 * master)
    return (input_grad.reshape(1, 2, 256, 2048), new_weight[None], new_moment1[None], new_moment2[None])


def solution(mesh):
    return jax.shard_map(
        per_device,
        mesh=mesh,
        in_specs=(
            P("section", None, "dp", "mp"),
            P(None, "dp", "mp"),
            P("section", "mp", "dp"),
            P("section", "mp", "dp"),
            P("section", "mp", "dp"),
        ),
        out_specs=(
            P("section", None, "dp", "mp"),
            P("section", "mp", "dp"),
            P("section", "mp", "dp"),
            P("section", "mp", "dp"),
        ),
        check_vma=False,
    )
```

time: 1300 us -> 158 us (0.12)
  waiting for transfers between devices: 1150 us -> 0 us
  Pallas kernels: 0 us -> 150 us
  blocking collectives: 64.4 us -> 0 us
  matrix products: 47.5 us -> 0 us
  between operations: 14.5 us -> 0.66 us
    reduce_scatter x1 -> x0, waiting for transfers between devices: 710 us -> none  [per_device(): lax.psum_scatter(jnp.einsum('mtj,mti->ji', features, activations, preferr...]
    all_gather x3 -> x0, waiting for transfers between devices: 400 us -> none  [the longest x1 363 us: per_device(): lax.all_gather(master_weight[0].astype(jnp.bfloat16), 'dp', axis=1, tiled...]
    pallas_call x0 -> x1, Pallas kernels: none -> 150 us  [per_device(): pl.pallas_call(kernel, out_shape=(jax.ShapeDtypeStruct((512, 2048), BF),...]
    psum x1 -> x0, blocking collectives: 64.4 us -> none  [per_device(): lax.psum(jnp.sum(grad_shard * grad_shard), ('section', 'dp', 'mp'))]
    dot_general x3 -> x0, matrix products: 47.5 us -> none  [the longest x2 30 us: per_device(): jnp.einsum('mtj,ij->mti', features, weight_rows, preferred_element_type=j...]
    ppermute x1 -> x0, waiting for transfers between devices: 43.8 us -> none  [from_behind(): return lax.ppermute(block, axis, route)]
  transfers between devices with their start and end apart: 5 -> 0, of which waited for: 5 -> 0; matrix products, arithmetic and copies ran while one was open for 0% -> 0% of each run, Pallas kernels for 0% -> 0%
where the time goes in v2:
time: 158 us; the launch traced here: 157 us
  Pallas kernels  150 us (95%)
  other arithmetic  4.44 us (3%)
    pallas_call x1, Pallas kernels, per_device(): pl.pallas_call(kernel, out_shape=(jax.ShapeDtypeStruct((512, 2048), BF),...  150 us
    broadcast_in_dim x1, other arithmetic, per_device(): new_moment2[None]  4.44 us

profile of v2, /device:TPU:6, one launch (start us, length us, event | category | flops | bytes accessed | tf_op | source)
XLA Modules:
  0.0 156.7 jit_solution(10370072099144307750)
XLA Ops:
  0.6 0.0 copy-start
  0.6 150.3 %shard_map.84 = (bf16[512,2048]{1,0:T(8,128)(2,1)}, f32[2048,128]{1,0:T(8,128)}) custom-call(bf16[512,2048]{1,0:T(8,128)(2,1)} %bitcast.24, bf16[512,2048]{1,0:T(8,128)(2,1)} %bitcast.25, f32[2048,128]{1,0:T(8,128)} %bitcast.23), custom_call_target="tpu_custom_call" | custom-call | tf_op jit(solution)/shard_map/pallas_call | solution.py:604
  150.9 0.0 copy-done
  150.9 0.0 copy-start.1
  150.9 4.4 %fusion.2 = (f32[1,2048,128]{2,1,0:T(8,128)}, f32[1,2048,128]{2,1,0:T(8,128)}, f32[1,2048,128]{2,1,0:T(8,128)}) fusion(f32[2048,128]{1,0:T(8,128)} %get-tuple-element.7, f32[1,2048,128]{2,1,0:T(8,128)} %param.9, f32[1,2048,128]{2,1,0:T(8,128)} %param.8, f32[1,2048,128]{2,1,0:T(8,128)S(1)} %copy-done), kind=kLoop, calls=%fused_computation.5 | loop fusion | flops 3932160 | bytes 7340032 | tf_op jit(solution)/shard_map/broadcast_in_dim | solution.py:648
  155.4 0.0 copy-done.1
  155.4 1.3 copy.10
Async XLA Ops:
  0.6 150.3 %copy-start = (f32[1,2048,128]{2,1,0:T(8,128)S(1)}, f32[1,2048,128]{2,1,0:T(8,128)}, u32[]{:S(2)}) copy-start(f32[1,2048,128]{2,1,0:T(8,128)} %param.7) | copy-start | bytes 3145732
  150.9 4.5 %copy-start.1 = (bf16[512,2048]{1,0:T(8,128)(2,1)S(1)}, bf16[512,2048]{1,0:T(8,128)(2,1)}, u32[]{:S(2)}) copy-start(bf16[512,2048]{1,0:T(8,128)(2,1)} %get-tuple-element.6) | copy-start | bytes 6291460

commit v3 on v2

--- a/solution.py
+++ b/solution.py
@@ -8,7 +8,7 @@
 MESH = pl.DeviceIdType.MESH
 BF = jnp.bfloat16
 F32 = jnp.float32
-X_X, G_X, G_CUT, G_CORE, G_CORE2, G_CORE3, D_CUT, D_CORE, P_X, O_X, F_X, W_X = 0, 1, 2, 3, 4, 5, 6, 14, 22, 26, 27, 28
+X_X, G_X, G_CUT, G_CORE, G_CORE2, G_CORE3, D_CUT, D_CORE, P_X, O_X, F_X, W_X = 0, 1, 2, 3, 4, 5, 6, 14, 22, 26, 27, 31
 
 
 def dot_nt(a, b):
@@ -19,17 +19,32 @@
     return jnp.dot(a, b, preferred_element_type=F32)
 
 
-def low_lanes(a, b):
-    return jnp.where(lax.broadcasted_iota(jnp.int32, a.shape, 1) < 64, a, pltpu.roll(b, 64, 1))
-
-
-def high_lanes(a, b):
-    return jnp.where(lax.broadcasted_iota(jnp.int32, a.shape, 1) < 64, pltpu.roll(a, 64, 1), b)
+def lane_group(x):
+    return lax.broadcasted_iota(jnp.int32, x.shape, 1) // 32
+
+
+def merge(parts, take):
+    out = None
+    for a, part in enumerate(parts):
+        moved = pltpu.roll(part, (32 * (a - take(a))) % 128, 1)
+        out = moved if out is None else jnp.where(lane_group(part) == a, moved, out)
+    return out
+
+
+def transpose(parts):
+    g = lane_group(parts[0])
+    even, odd = g % 2 == 0, g < 2
+    a, b, c, d = parts
+    a, b = jnp.where(even, a, pltpu.roll(b, 32, 1)), jnp.where(even, pltpu.roll(a, 96, 1), b)
+    c, d = jnp.where(even, c, pltpu.roll(d, 32, 1)), jnp.where(even, pltpu.roll(c, 96, 1), d)
+    a, c = jnp.where(odd, a, pltpu.roll(c, 64, 1)), jnp.where(odd, pltpu.roll(a, 64, 1), c)
+    b, d = jnp.where(odd, b, pltpu.roll(d, 64, 1)), jnp.where(odd, pltpu.roll(b, 64, 1), d)
+    return a, b, c, d
 
 
 def kernel(
     x_hbm, g_hbm, w_ref, out_ref, grad_ref,
-    Wg, Wx, Gv, D, Dp, Xo, Xp, XT, S, Ra, Rb, Rc, Rd, T, Tf, F, Fp, acc, Nb,
+    Wg, Wx, Gv, D, Dp, Xo, Xp, XT, S, Ra, Rb, Rc, Rd, T, Tf, F, Fp, acc, Own, Nb,
     ldx, ldg, ag_s, ag_r, rs_s, rs_r, ms, mr, ns, nr,
 ):
     s = lax.axis_index("section")
@@ -77,22 +92,23 @@
         for i in range(4, 8):
             gload(i, Gv.at[0, 8 + i]).start()
 
-    @pl.when(above)
-    def _():
-        for a in range(16):
-            b, r = a // 8, a % 8
-            Wg[z, y, p, 64 * a : 64 * a + 64] = w_ref[pl.ds(256 * r + 128 * u + 64 * b, 64), :].astype(BF)
-            Wx[64 * a : 64 * a + 64] = w_ref[pl.ds(256 * r + 128 * (1 - u) + 64 * b, 64), :].astype(BF)
-
-    @pl.when(below)
-    def _():
-        for r in range(8):
-            Wg[z, y, r // 4, 256 * (r % 4) : 256 * (r % 4) + 256] = w_ref[256 * r : 256 * r + 256, :].astype(BF)
-
     barrier = pltpu.get_barrier_semaphore()
     peers = [zdev(1), zdev(2), zdev(3), ydev(1), ydev(2), ydev(3), *near]
     for to in peers:
         pl.semaphore_signal(barrier, inc=1, device_id=to, device_id_type=MESH)
+
+    @pl.when(above)
+    def _():
+        for a in range(32):
+            rows = 256 * (a % 8) + 32 * (a // 8)
+            Wg[z, y, p, 32 * a : 32 * a + 32] = w_ref[pl.ds(rows + 128 * u, 32), :].astype(BF)
+            Wx[32 * a : 32 * a + 32] = w_ref[pl.ds(rows + 128 * (1 - u), 32), :].astype(BF)
+
+    @pl.when(below)
+    def _():
+        for r in range(8):
+            Wg[z, y, r // 4, 256 * (r % 4) : 256 * (r % 4) + 256] = w_ref[256 * r : 256 * r + 256, :].astype(BF)
+
     pl.semaphore_wait(barrier, len(peers))
 
     def w_x(k):
@@ -201,96 +217,10 @@
             part = dot_nt(left, right)
             acc[...] = part if zz == 0 else acc[...] + part
         for rr in range(2):
-            q = 8 * c + 4 * (k % 2) + 2 * rr
-            g0 = Gv[t, q, :, pl.ds(128 * u, 128)].astype(F32)
-            g1 = Gv[t, q + 1, :, pl.ds(128 * u, 128)].astype(F32)
-            mine = jnp.where(k < 2, low_lanes(g0, g1), high_lanes(g0, g1))
+            mine = [Gv[t, 8 * c + 4 * rr + a, :, pl.ds(128 * u, 128)].astype(F32) for a in range(4)]
+            mine = merge(mine, lambda a: k)
             D[8 * c + 2 * k + rr, pl.ds(512 * t, 512)] = (acc[:, 128 * rr : 128 * rr + 128] + mine).astype(BF)
         d_cut(k, j).start()
-
-    gather_begin(0)
-    gather_begin(1)
-
-    @pl.loop(0, 12)
-    def _(i):
-        @pl.when(i < 6)
-        def _():
-            gather_begin(i + 2)
-
-        @pl.when(i < 8)
-        def _():
-            gather_on(0, i)
-
-        @pl.when((i >= 1) & (i < 9))
-        def _():
-            gather_end(0, i - 1)
-            gather_rows(i - 1)
-
-        @pl.when((i >= 3) & (i < 11))
-        def _():
-            gather_on(1, i - 3)
-
-        @pl.when(i >= 4)
-        def _():
-            gather_end(1, i - 4)
-
-        @pl.when(i == 4)
-        def _():
-            for j in range(16):
-                xload(j).wait()
-
-            @pl.when(below)
-            def _():
-                x_full.start()
-
-                @pl.loop(0, 16)
-                def _(j):
-                    XT[pl.ds(128 * j, 128), pl.ds(512 * p, 512)] = Xo[j // 2, j % 2].T
-
-            @pl.when(above)
-            def _():
-                g_core_in.wait_recv()
-
-                @pl.loop(0, 8)
-                def _(r):
-                    XT[pl.ds(128 * r, 128), pl.ds(512 * p, 512)] = Xo[r, u].T
-
-        @pl.when(above & (i >= 5) & (i % 2 == 1))
-        def _():
-            k = (i - 5) // 2
-            layer_unit(k, 0)
-
-            @pl.when(k == 0)
-            def _():
-                g_x_in.wait_recv()
-                g_core2.start()
-                x_half.start()
-                g_cut_in.wait_recv()
-                g_core3.start()
-                g_core2_in.wait_recv()
-                g_core3_in.wait_recv()
-
-            @pl.when(k < 2)
-            def _():
-                layer_unit(k, 1)
-
-        @pl.when(below & ((i == 9) | (i == 11)))
-        def _():
-            d_on((i - 9) // 2, 0)
-            d_on((i - 9) // 2, 1)
-
-    @pl.when(above)
-    def _():
-        @pl.loop(2, 4)
-        def _(k):
-            layer_unit(k, 1)
-
-        rc(D.at[pl.ds(8 * c, 8), pl.ds(512 * (1 - p), 512)], Dp, O_X, pair).start()
-        x_half_in.wait_recv()
-
-        @pl.loop(0, 8)
-        def _(r):
-            XT[pl.ds(128 * r, 128), pl.ds(512 * (1 - p), 512)] = Xp[r, u].T
 
     LOW, HIGH, ALL = pl.ds(0, 128), pl.ds(128, 128), pl.ds(0, 256)
 
@@ -348,6 +278,10 @@
 
             reduce_start(1, m, h)
 
+    def f_x(m):
+        rows = pl.ds(2 * m, 2)
+        return rc(F.at[1 - p, rows], Fp.at[rows], F_X + m, pair)
+
     def finish(m):
         for h in range(2):
             for i in range(2, 6):
@@ -357,16 +291,20 @@
             F[h, 2 * m + 1] = v[128:]
             Nb[0, 0] = Nb[0, 0] + jnp.sum((v * v).reshape(32, 8, 128), axis=0)
 
-    def input_part(n, t):
+        @pl.when(above)
+        def _():
+            f_x(m).start()
+
+    def input_part(n, t, to):
         for zz in range(4):
             left = jnp.concatenate([Gv[t, 8 + 2 * zz], Gv[t, 9 + 2 * zz]], axis=1)
             right = jnp.concatenate(
                 [Wg[zz, yy, n // 4, pl.ds(256 * (n % 4), 256), :] for yy in range(4)], axis=1)
             part = dot_nt(left, right)
-            acc[...] = part if zz == 0 else acc[...] + part
+            to[...] = part if zz == 0 else to[...] + part
         lanes = pl.ds(128 * p, 128)
         mine = Gv[t, 8 + 4 * c + n // 2, :, pl.ds(pl.multiple_of(128 * (n % 2), 128), 128)]
-        acc[:, lanes] = acc[:, lanes] + mine.astype(F32)
+        to[:, lanes] = to[:, lanes] + mine.astype(F32)
 
     def p_x(i):
         return rc(Gv.at[0, pl.ds(2 * i, 2)], Gv.at[1, pl.ds(2 * i, 2)], P_X + i, pair)
@@ -380,56 +318,145 @@
             S[m, q // 4, q % 4, 1] = v[:, 128:].astype(BF)
 
     def weight_grad_part(k):
-        @pl.loop(0, 8)
+        @pl.loop(0, 4)
         def _(i):
-            cc, m = i // 4, i % 4
+            cc, half = i // 2, i % 2
             right = jnp.concatenate([D[8 * cc + 2 * k], D[8 * cc + 2 * k + 1]], axis=1)
-            v = [dot_nn(XT[pl.ds(1024 * h + 256 * m, 256), 0:1024], right) for h in range(2)]
+            v = [dot_nn(XT[pl.ds(512 * g + 256 * half, 256), 0:1024], right) for g in range(4)]
             for rr in range(2):
-                v0, v1 = (a[:, 128 * rr : 128 * rr + 128] for a in v)
-                to = S.at[2 * (k // 2) + m // 2, 2 * cc + k % 2]
-                to[2 * rr, m % 2] = low_lanes(v0, v1).astype(BF)
-                to[2 * rr + 1, m % 2] = high_lanes(v0, v1).astype(BF)
+                for a, b in enumerate(transpose([x[:, 128 * rr : 128 * rr + 128] for x in v])):
+                    S[k, 2 * cc + rr, a, half] = b.astype(BF)
+
+    def weight_grad_from(k):
+        @pl.when(k < 2)
+        def _():
+            d_core_in(k, 0).wait_recv()
+
+        d_core_in(k, 1).wait_recv()
+        weight_grad_part(k)
+        first_reduce(k)
 
     def natural(t):
-        @pl.loop(0, 8)
-        def _(a):
-            b0, b1 = 8 * (a // 4) + a % 4, 8 * (a // 4) + 4 + a % 4
-            v0 = D[b0, pl.ds(512 * t, 512)].astype(F32)
-            v1 = D[b1, pl.ds(512 * t, 512)].astype(F32)
-            Gv[t, 8 + a, :, 0:128] = low_lanes(v0, v1).astype(BF)
-            Gv[t, 8 + a, :, 128:256] = high_lanes(v0, v1).astype(BF)
+        @pl.loop(0, 4)
+        def _(i):
+            b = 8 * (i // 2) + i % 2
+            v = transpose([D[b + 2 * g, pl.ds(512 * t, 512)].astype(F32) for g in range(4)])
+            for a in range(4):
+                Gv[t, 8 + 2 * i + a // 2, :, 128 * (a % 2) : 128 * (a % 2) + 128] = v[a].astype(BF)
 
     def partner_part(i):
         @pl.loop(0, 2)
         def _(j):
-            input_part(2 * i + j, 1 - p)
+            input_part(2 * i + j, 1 - p, acc)
             Gv[0, 2 * i + j] = acc[...].astype(BF)
 
-        p_x(i).start()
-
     def first_reduce(m):
         for h in range(2):
             reduce_start(0, m, h)
 
+    gather_begin(0)
+    gather_begin(1)
+
+    @pl.loop(0, 12)
+    def _(i):
+        @pl.when(i < 6)
+        def _():
+            gather_begin(i + 2)
+
+        @pl.when(i < 8)
+        def _():
+            gather_on(0, i)
+
+        @pl.when((i >= 1) & (i < 9))
+        def _():
+            gather_end(0, i - 1)
+            gather_rows(i - 1)
+
+        @pl.when((i >= 3) & (i < 11))
+        def _():
+            gather_on(1, i - 3)
+
+        @pl.when(i >= 4)
+        def _():
+            gather_end(1, i - 4)
+
+        @pl.when(i == 4)
+        def _():
+            for j in range(16):
+                xload(j).wait()
+
+            @pl.when(below)
+            def _():
+                x_full.start()
+
+                @pl.loop(0, 16)
+                def _(j):
+                    XT[pl.ds(128 * j, 128), pl.ds(512 * p, 512)] = Xo[j // 2, j % 2].T
+
+            @pl.when(above)
+            def _():
+                g_core_in.wait_recv()
+
+                @pl.loop(0, 8)
+                def _(r):
+                    XT[pl.ds(128 * r, 128), pl.ds(512 * p, 512)] = Xo[r, u].T
+
+        @pl.when(above & (i >= 5) & (i % 2 == 1))
+        def _():
+            k = (i - 5) // 2
+            layer_unit(k, 0)
+
+            @pl.when(k == 0)
+            def _():
+                g_x_in.wait_recv()
+                g_core2.start()
+                x_half.start()
+                g_cut_in.wait_recv()
+                g_core3.start()
+                g_core2_in.wait_recv()
+                g_core3_in.wait_recv()
+
+            @pl.when(k < 2)
+            def _():
+                layer_unit(k, 1)
+
+        @pl.when(above & (i == 10))
+        def _():
+            x_half_in.wait_recv()
+
+            @pl.loop(0, 8)
+            def _(r):
+                XT[pl.ds(128 * r, 128), pl.ds(512 * (1 - p), 512)] = Xp[r, u].T
+
+            weight_grad(0)
+            first_reduce(0)
+
+        @pl.when(below & ((i == 9) | (i == 11)))
+        def _():
+            d_on((i - 9) // 2, 0)
+            d_on((i - 9) // 2, 1)
+
+        @pl.when(below & (i == 10))
+        def _():
+            x_full.wait_recv()
+
+            @pl.loop(0, 16)
+            def _(j):
+                XT[pl.ds(128 * j, 128), pl.ds(512 * (1 - p), 512)] = Xp[j // 2, j % 2].T
+
+        @pl.when(below & (i >= 10))
+        def _():
+            weight_grad_from(i - 10)
+
+    @pl.when(above)
+    def _():
+        @pl.loop(2, 4)
+        def _(k):
+            layer_unit(k, 1)
+
+        rc(D.at[pl.ds(8 * c, 8), pl.ds(512 * (1 - p), 512)], Dp, O_X, pair).start()
     @pl.when(below)
     def _():
-        x_full.wait_recv()
-
-        @pl.loop(0, 16)
-        def _(i):
-            XT[pl.ds(128 * i, 128), pl.ds(512 * (1 - p), 512)] = Xp[i // 2, i % 2].T
-
-        @pl.loop(0, 2)
-        def _(k):
-            d_core_in(k, 0).wait_recv()
-            d_core_in(k, 1).wait_recv()
-            weight_grad_part(k)
-
-        @pl.loop(0, 2)
-        def _(m):
-            first_reduce(m)
-
         g_cut.wait_send()
 
         @pl.loop(2, 4)
@@ -442,24 +469,20 @@
 
         natural(1 - p)
 
-        @pl.loop(0, 2)
-        def _(i):
-            partner_part(2 * i)
-            partner_part(2 * i + 1)
-            reduce_on(0, i)
+        partner_part(0)
+        p_x(0).start()
 
         @pl.loop(2, 4)
         def _(k):
             d_on(k, 1)
-
-        @pl.loop(2, 4)
-        def _(k):
-            d_core_in(k, 1).wait_recv()
-            weight_grad_part(k)
-
-        @pl.loop(2, 4)
-        def _(m):
-            first_reduce(m)
+            weight_grad_from(k)
+            partner_part(k - 1)
+            p_x(k - 1).start()
+
+        partner_part(3)
+        p_x(3).start()
+        reduce_on(0, 0)
+        reduce_on(0, 1)
 
         natural(p)
 
@@ -467,7 +490,7 @@
 
     @pl.loop(0, 8)
     def _(i):
-        @pl.when(above & (i < 4))
+        @pl.when(above & (i >= 1) & (i < 4))
         def _():
             weight_grad(i)
             first_reduce(i)
@@ -488,22 +511,17 @@
         def _():
             finish(i - 4)
 
-    f_x = rc(F.at[1 - p], Fp, F_X, pair)
-
-    @pl.when(above)
-    def _():
-        f_x.start()
+        @pl.when(below & (i >= 2) & (i < 6))
+        def _():
+            for j in range(2):
+                input_part(2 * (i - 2) + j, p, Own.at[2 * (i - 2) + j])
 
     def own_part(i):
         @pl.when(below)
         def _():
             p_x(i).wait_recv()
-
-            @pl.loop(0, 2)
-            def _(j):
-                n = 2 * i + j
-                input_part(n, p)
-                out_ref[:, pl.ds(pl.multiple_of(256 * n, 256), 256)] = (acc[...] + Gv[1, n].astype(F32)).astype(BF)
+            for n in (2 * i, 2 * i + 1):
+                out_ref[:, 256 * n : 256 * n + 256] = (Own[n] + Gv[1, n].astype(F32)).astype(BF)
 
     steps = [near, [ydev(1), ydev(3), ydev(2)], [zdev(1), zdev(3), zdev(2)]]
     for i, targets in enumerate(steps):
@@ -513,7 +531,6 @@
             for j, to in enumerate(targets)]
         for copy in copies:
             copy.start()
-        own_part(i)
         for copy in copies:
             copy.wait_recv()
         v = Nb[i, 0]
@@ -530,34 +547,35 @@
 
     @pl.when(above)
     def _():
-        f_x.wait_recv()
+        for m in range(4):
+            f_x(m).wait_recv()
         for r in range(8):
             grad_ref[pl.ds(256 * r + 128 * u, 128), :] = F[p, r] * clip
             grad_ref[pl.ds(256 * r + 128 * (1 - u), 128), :] = Fp[r] * clip
 
     @pl.when(below)
     def _():
-        for r in range(8):
-            m, half = r // 2, r % 2
-            a, b = F[m % 2, 2 * (m // 2) + half], F[m % 2, 4 + 2 * (m // 2) + half]
-            grad_ref[128 * r : 128 * r + 128, :] = low_lanes(a, b) * clip
-            grad_ref[1024 + 128 * r : 1152 + 128 * r, :] = high_lanes(a, b) * clip
-
-    own_part(3)
+        for r in range(4):
+            half, low = r // 2, r % 2
+            v = transpose([F[half, 2 * k + low] for k in range(4)])
+            for g in range(4):
+                rows = 512 * g + 256 * half + 128 * low
+                grad_ref[rows : rows + 128, :] = v[g] * clip
+
+    for i in range(4):
+        own_part(i)
 
     @pl.when(above)
     def _():
         rc(Dp, Dp, O_X, pair).wait_recv()
 
-        @pl.loop(0, 4)
-        def _(a):
-            for v0, v1, par in (
-                (D[8 * c + a, pl.ds(512 * p, 512)], D[8 * c + 4 + a, pl.ds(512 * p, 512)], u),
-                (Dp[a], Dp[4 + a], 1 - u),
-            ):
-                v0, v1 = v0.astype(F32), v1.astype(F32)
-                out_ref[:, pl.ds(pl.multiple_of(512 * a + 128 * par, 128), 128)] = low_lanes(v0, v1).astype(BF)
-                out_ref[:, pl.ds(pl.multiple_of(512 * a + 256 + 128 * par, 128), 128)] = high_lanes(v0, v1).astype(BF)
+        @pl.loop(0, 2)
+        def _(i):
+            for par, src in ((u, D.at[pl.ds(8 * c, 8), pl.ds(512 * p, 512)]), (1 - u, Dp)):
+                v = transpose([src[2 * g + i].astype(F32) for g in range(4)])
+                for a in range(4):
+                    lanes = pl.ds(pl.multiple_of(1024 * i + 256 * a + 128 * par, 128), 128)
+                    out_ref[:, lanes] = v[a].astype(BF)
 
     @pl.loop(0, 8)
     def _(k):
@@ -575,8 +593,10 @@
 
     @pl.when(above)
     def _():
-        for copy in (g_x, g_core, g_core2, g_core3, x_half, f_x):
+        for copy in (g_x, g_core, g_core2, g_core3, x_half):
             copy.wait_send()
+        for m in range(4):
+            f_x(m).wait_send()
         for k in range(8):
             w_x(k).wait_send()
         rc(Dp, Dp, O_X, pair).wait_send()
@@ -594,7 +614,9 @@
         def _(k):
             d_core(k, 0).wait_send()
             d_core(k, 1).wait_send()
-            p_x(k).wait_send()
+
+        for i in range(4):
+            p_x(i).wait_send()
 
 
 def per_device(saved_input, out_grad, master_weight, moment1, moment2):
@@ -628,11 +650,12 @@
             pltpu.VMEM((2, 8, 128, 128), F32),
             pltpu.VMEM((8, 128, 128), F32),
             pltpu.VMEM((512, 256), F32),
+            pltpu.VMEM((8, 512, 256), F32),
             pltpu.VMEM((3, 8, 8, 128), F32),
             dma((16,)), dma((8,)),
             dma((2, 8, 2, 4)), dma((2, 8, 2, 4)),
             dma((2, 4, 2, 6)), dma((2, 4, 2, 6)),
-            dma((36,)), dma((36,)),
+            dma((39,)), dma((39,)),
             dma((3, 7)), dma((3, 7)),
         ],
         compiler_params=pltpu.CompilerParams(

time: 158 us -> 156 us (0.987)
  no operation moved by 1% of the time
where the time goes in v3:
time: 156 us
  Pallas kernels  149 us (96%)
  other arithmetic  4.44 us (3%)
    pallas_call x1, Pallas kernels, per_device(): pl.pallas_call(kernel, out_shape=(jax.ShapeDtypeStruct((512, 2048), BF),...  149 us
    broadcast_in_dim x1, other arithmetic, per_device(): new_moment2[None]  4.44 us

profile of v3, /device:TPU:6, one launch (start us, length us, event | category | flops | bytes accessed | tf_op | source)
XLA Modules:
  0.0 155.7 jit_solution(9253320794678139147)
XLA Ops:
  0.6 0.0 copy-start
  0.6 149.2 %shard_map.84 = (bf16[512,2048]{1,0:T(8,128)(2,1)}, f32[2048,128]{1,0:T(8,128)}) custom-call(bf16[512,2048]{1,0:T(8,128)(2,1)} %bitcast.24, bf16[512,2048]{1,0:T(8,128)(2,1)} %bitcast.25, f32[2048,128]{1,0:T(8,128)} %bitcast.23), custom_call_target="tpu_custom_call" | custom-call | tf_op jit(solution)/shard_map/pallas_call | solution.py:626
  149.9 0.0 copy-done
  149.9 0.0 copy-start.1
  149.9 4.4 %fusion.2 = (f32[1,2048,128]{2,1,0:T(8,128)}, f32[1,2048,128]{2,1,0:T(8,128)}, f32[1,2048,128]{2,1,0:T(8,128)}) fusion(f32[2048,128]{1,0:T(8,128)} %get-tuple-element.7, f32[1,2048,128]{2,1,0:T(8,128)} %param.9, f32[1,2048,128]{2,1,0:T(8,128)} %param.8, f32[1,2048,128]{2,1,0:T(8,128)S(1)} %copy-done), kind=kLoop, calls=%fused_computation.5 | loop fusion | flops 3932160 | bytes 7340032 | tf_op jit(solution)/shard_map/broadcast_in_dim | solution.py:671
  154.3 0.0 copy-done.1
  154.3 1.3 copy.10
Async XLA Ops:
  0.6 149.2 %copy-start = (f32[1,2048,128]{2,1,0:T(8,128)S(1)}, f32[1,2048,128]{2,1,0:T(8,128)}, u32[]{:S(2)}) copy-start(f32[1,2048,128]{2,1,0:T(8,128)} %param.7) | copy-start | bytes 3145732
  149.9 4.5 %copy-start.1 = (bf16[512,2048]{1,0:T(8,128)(2,1)S(1)}, bf16[512,2048]{1,0:T(8,128)(2,1)}, u32[]{:S(2)}) copy-start(bf16[512,2048]{1,0:T(8,128)(2,1)} %get-tuple-element.6) | copy-start | bytes 6291460

commit v4 on v3

--- a/solution.py
+++ b/solution.py
@@ -79,18 +79,18 @@
     def gload(i, dst):
         return pltpu.make_async_copy(g_hbm.at[:, pl.ds(256 * i, 256)], dst, ldg.at[i])
 
+    @pl.when(above)
+    def _():
+        for i in range(8):
+            gload(i, Gv.at[p, 8 * c + i]).start()
+
+    @pl.when(below)
+    def _():
+        for i in range(4, 8):
+            gload(i, Gv.at[0, 8 + i]).start()
+
     for i in range(16):
         xload(i).start()
-
-    @pl.when(above)
-    def _():
-        for i in range(8):
-            gload(i, Gv.at[p, 8 * c + i]).start()
-
-    @pl.when(below)
-    def _():
-        for i in range(4, 8):
-            gload(i, Gv.at[0, 8 + i]).start()
 
     barrier = pltpu.get_barrier_semaphore()
     peers = [zdev(1), zdev(2), zdev(3), ydev(1), ydev(2), ydev(3), *near]
@@ -159,16 +159,6 @@
     def _():
         for k in range(8):
             w_x(k).start()
-        for i in range(8):
-            gload(i, Gv.at[p, 8 * c + i]).wait()
-        g_x.start()
-        g_core.start()
-
-    @pl.when(below)
-    def _():
-        for i in range(4, 8):
-            gload(i, Gv.at[0, 8 + i]).wait()
-        g_cut.start()
 
     def gather_begin(k):
         @pl.when(above)
@@ -355,6 +345,20 @@
             reduce_start(0, m, h)
 
     gather_begin(0)
+
+    @pl.when(above)
+    def _():
+        for i in range(8):
+            gload(i, Gv.at[p, 8 * c + i]).wait()
+        g_x.start()
+        g_core.start()
+
+    @pl.when(below)
+    def _():
+        for i in range(4, 8):
+            gload(i, Gv.at[0, 8 + i]).wait()
+        g_cut.start()
+
     gather_begin(1)
 
     @pl.loop(0, 12)
@@ -471,6 +475,7 @@
 
         partner_part(0)
         p_x(0).start()
+        reduce_on(0, 0)
 
         @pl.loop(2, 4)
         def _(k):
@@ -479,10 +484,13 @@
             partner_part(k - 1)
             p_x(k - 1).start()
 
+            @pl.when(k == 2)
+            def _():
+                reduce_on(0, 1)
+
+        row_sums(0)
         partner_part(3)
         p_x(3).start()
-        reduce_on(0, 0)
-        reduce_on(0, 1)
 
         natural(p)
 
@@ -499,7 +507,7 @@
         def _():
             reduce_on(0, i - 1)
 
-        @pl.when((i >= 2) & (i < 6))
+        @pl.when((i >= 2) & (i < 6) & (above | (i >= 3)))
         def _():
             row_sums(i - 2)
 

time: 156 us -> 156 us (level)
  no operation moved by 1% of the time
where the time goes in v4:
time: 156 us
  Pallas kernels  149 us (96%)
  other arithmetic  4.44 us (3%)
    pallas_call x1, Pallas kernels, per_device(): pl.pallas_call(kernel, out_shape=(jax.ShapeDtypeStruct((512, 2048), BF),...  149 us
    broadcast_in_dim x1, other arithmetic, per_device(): new_moment2[None]  4.44 us

profile of v4, /device:TPU:6, one launch (start us, length us, event | category | flops | bytes accessed | tf_op | source)
XLA Modules:
  0.0 155.7 jit_solution(13052501844428518722)
XLA Ops:
  0.6 0.0 copy-start
  0.6 149.2 %shard_map.84 = (bf16[512,2048]{1,0:T(8,128)(2,1)}, f32[2048,128]{1,0:T(8,128)}) custom-call(bf16[512,2048]{1,0:T(8,128)(2,1)} %bitcast.24, bf16[512,2048]{1,0:T(8,128)(2,1)} %bitcast.25, f32[2048,128]{1,0:T(8,128)} %bitcast.23), custom_call_target="tpu_custom_call" | custom-call | tf_op jit(solution)/shard_map/pallas_call | solution.py:634
  149.9 0.0 copy-done
  149.9 0.0 copy-start.1
  149.9 4.4 %fusion.2 = (f32[1,2048,128]{2,1,0:T(8,128)}, f32[1,2048,128]{2,1,0:T(8,128)}, f32[1,2048,128]{2,1,0:T(8,128)}) fusion(f32[2048,128]{1,0:T(8,128)} %get-tuple-element.7, f32[1,2048,128]{2,1,0:T(8,128)} %param.9, f32[1,2048,128]{2,1,0:T(8,128)} %param.8, f32[1,2048,128]{2,1,0:T(8,128)S(1)} %copy-done), kind=kLoop, calls=%fused_computation.5 | loop fusion | flops 3932160 | bytes 7340032 | tf_op jit(solution)/shard_map/broadcast_in_dim | solution.py:679
  154.3 0.0 copy-done.1
  154.3 1.3 copy.10
Async XLA Ops:
  0.6 149.2 %copy-start = (f32[1,2048,128]{2,1,0:T(8,128)S(1)}, f32[1,2048,128]{2,1,0:T(8,128)}, u32[]{:S(2)}) copy-start(f32[1,2048,128]{2,1,0:T(8,128)} %param.7) | copy-start | bytes 3145732
  149.9 4.5 %copy-start.1 = (bf16[512,2048]{1,0:T(8,128)(2,1)S(1)}, bf16[512,2048]{1,0:T(8,128)(2,1)}, u32[]{:S(2)}) copy-start(bf16[512,2048]{1,0:T(8,128)(2,1)} %get-tuple-element.6) | copy-start | bytes 6291460
